TPU v7x, 32 devices: a whole 2x2x4 slice. The times are simulated.
32 devices in a mesh: dp: 8 (over z, y), rep: 4 (over x, core).
Axes of the slice: x: 2, y: 2, z: 4, core: 2. Of those that a mesh axis runs over, the one named last changes fastest.
Arguments:
- q_raw: bfloat16 [3, 96, 8192], P(None, 'dp', 'rep'), may hold values from -16 to 16
- k_raw: bfloat16 [3, 96, 512], P(None, 'dp', 'rep'), may hold values from -8 to 8
- v_raw: bfloat16 [3, 96, 512], P(None, 'dp', 'rep'), may hold values from -6 to 6
- q_gain: float32 [128], replicated, may hold values from 0.6 to 5.5
- k_gain: float32 [128], replicated, may hold values from 0.6 to 5.5
- kv_pool: bfloat16 [384, 64, 2, 512], P('dp', None, None, 'rep'), may hold values from -6 to 6
- page_table: int32 [96, 4], P('dp'), may hold values from 0 to 47, as said below
- cache_len: int32 [96], P('dp'), may hold values from 1 to 253, as said below
- out_pages: int32 [64], P('dp'), may hold values from 0 to 47, as said below
- in_slots: int32 [64], P('dp'), may hold values from 0 to 47, as said below
- hidden_in: bfloat16 [3, 96, 4096], P(None, 'dp', 'rep'), may hold values from -48 to 48
- ln_gain: float32 [4096], replicated, may hold values from 0.1 to 1.9
- route_ids: int32 [3, 96, 8], P(None, 'dp'), may hold values from 0 to 63, all different within a row; in each aligned block of 12 rows (0 to 11, 12 to 23, ..., all dimensions but the last counted through in order) at most 2 rows name the same one
- route_logits: float32 [3, 96, 8], P(None, 'dp'), may hold values from -4 to 4
- w_gate: bfloat16 [128, 4096, 512], P('dp', None, 'rep'), may hold values from -0.09375 to 0.09375
- w_up: bfloat16 [128, 4096, 512], P('dp', None, 'rep'), may hold values from -0.09375 to 0.09375
- w_down: bfloat16 [128, 512, 4096], P('dp', None, 'rep'), may hold values from -0.1875 to 0.1875
Outputs:
- attn_out: bfloat16 [3, 96, 8192], P(None, 'dp', 'rep')
- moe_out: bfloat16 [3, 96, 4096], P(None, 'dp', 'rep')
Inputs may be any that keep to these rules, and one draw needn't show every extreme that they name: `route_ids`: each row names 8 different experts; in each step the 12 rows of one dp index name no expert more than 2 times, a bound that some block reaches. `page_table`: the 12 rows of one dp index hold each page number of that index once. `cache_len`: the first request holds the most. `out_pages`: the 8 entries of one dp index are different pages. `in_slots`: the 8 entries of one dp index are different pages.
All inputs are finite; a program needn't handle non-finite values.
Results may differ from a plain program's by a relative error of at most 0.008.
Values may be sent and summed in bfloat16 or wider, within the bound.
No kernel may reach another device: no remote copies, remote signals or barrier semaphores. Data moves between devices by JAX's collectives and lax.ppermute only.
A program may use at most 128 MiB of HBM per device.

v0:
```python
import math

import jax
import jax.numpy as jnp
from jax import lax
from jax.sharding import PartitionSpec as P

D = 4096
HEAD_DIM = 128
EXPERTS = 64
STEPS = 3
CAPACITY = 2


EPS = 1e-06
THETA = 1000000.0


def from_behind(x, axis, by):
    size = lax.axis_size(axis)
    return lax.ppermute(x, axis, [(i, (i + by) % size) for i in range(size)])


def head_norm(values, gain):
    mean_square = jnp.mean(values * values, axis=-1, keepdims=True)
    return values * lax.rsqrt(mean_square + EPS) * gain


def rotate(values, position):
    half_dim = values.shape[-1] // 2
    exponent = jnp.arange(half_dim, dtype=jnp.float32) * (2.0 / values.shape[-1])
    frequency = THETA ** (-exponent)
    angle = position.astype(jnp.float32)[:, None] * frequency[None, :]
    cosine = jnp.cos(angle)[:, None, :]
    sine_part = jnp.sin(angle)[:, None, :]
    first_half = values[..., :half_dim]
    second_half = values[..., half_dim:]
    return jnp.concatenate(
        [
            first_half * cosine - second_half * sine_part,
            second_half * cosine + first_half * sine_part,
        ],
        axis=-1,
    )


def attend(context, lengths, queries_in, keys_in, values_in, q_gain, k_gain):
    row_count, span_len, _, kv_width = context.shape
    kv_count = kv_width // HEAD_DIM
    q_count = queries_in.shape[-1] // HEAD_DIM
    groups = q_count // kv_count
    places = jnp.arange(span_len, dtype=jnp.int32)
    scaling = 1.0 / math.sqrt(HEAD_DIM)
    results = []
    for step_index in range(STEPS):
        position = lengths + step_index
        queries = queries_in[step_index].astype(jnp.float32).reshape(row_count, q_count, HEAD_DIM)
        queries = rotate(head_norm(queries, q_gain), position).astype(jnp.bfloat16)
        new_keys = keys_in[step_index].astype(jnp.float32).reshape(row_count, kv_count, HEAD_DIM)
        new_keys = rotate(head_norm(new_keys, k_gain), position).astype(jnp.bfloat16)
        fresh_rows = jnp.stack(
            [new_keys.reshape(row_count, kv_width), values_in[step_index]], axis=1
        )
        landing = (places[None, :] == position[:, None])[:, :, None, None]
        context = jnp.where(landing, fresh_rows[:, None, :, :], context)
        key_rows = context[:, :, 0, :].reshape(row_count, span_len, kv_count, HEAD_DIM)
        value_rows = context[:, :, 1, :].reshape(row_count, span_len, kv_count, HEAD_DIM)
        grouped = queries.reshape(row_count, kv_count, groups, HEAD_DIM)
        scores = (
            jnp.einsum("rhgd,rshd->rhgs", grouped, key_rows, preferred_element_type=jnp.float32)
            * scaling
        )
        valid = (places[None, :] <= position[:, None])[:, None, None, :]
        scores = jnp.where(valid, scores, -1e30)
        row_top = jnp.max(scores, axis=-1, keepdims=True)
        expos = jnp.where(valid, jnp.exp(scores - row_top), 0.0)
        probs = (expos / jnp.sum(expos, axis=-1, keepdims=True)).astype(jnp.bfloat16)
        mixed = jnp.einsum("rhgs,rshd->rhgd", probs, value_rows, preferred_element_type=jnp.float32)
        results.append(mixed.reshape(row_count, q_count * HEAD_DIM).astype(jnp.bfloat16))
    return jnp.stack(results)


def place(route_ids):
    flat_ids = route_ids.reshape(route_ids.shape[0], -1)
    hot_table = (
        flat_ids[:, :, None] == jnp.arange(EXPERTS, dtype=jnp.int32)[None, None, :]
    ).astype(jnp.int32)
    before = jnp.cumsum(hot_table, axis=1) - hot_table
    return jnp.sum(before * hot_table, axis=2).reshape(route_ids.shape)


def local(
    q_raw,
    k_raw,
    v_raw,
    q_gain,
    k_gain,
    kv_pool,
    page_table,
    cache_len,
    out_pages,
    in_slots,
    hidden_in,
    ln_gain,
    route_ids,
    route_logits,
    w_gate,
    w_up,
    w_down,
):
    ranks = lax.axis_size("dp")
    leaving = kv_pool[out_pages]
    arriving = from_behind(leaving, "dp", ranks // 2)
    pool = kv_pool.at[in_slots].set(arriving)
    context = pool[page_table]
    row_count, page_count, page_len, kv_pair, kv_width = context.shape
    context = context.reshape(row_count, page_count * page_len, kv_pair, kv_width)
    attn_out = attend(context, cache_len, q_raw, k_raw, v_raw, q_gain, k_gain)
    whole_rows = lax.all_gather(hidden_in, "rep", axis=2, tiled=True)
    values = whole_rows.astype(jnp.float32)
    mean_square = jnp.mean(values * values, axis=-1, keepdims=True)
    normed = (values * lax.rsqrt(mean_square + EPS) * ln_gain).astype(jnp.bfloat16)
    slots = place(route_ids)
    targets = route_ids * CAPACITY + slots
    expert_slots = jnp.arange(EXPERTS * CAPACITY, dtype=jnp.int32)
    hits = jnp.any(targets[:, None, :, :] == expert_slots[None, :, None, None], axis=-1)
    hits = hits.astype(jnp.bfloat16).reshape(STEPS, EXPERTS, CAPACITY, row_count)
    packed = jnp.einsum("secr,srd->escd", hits, normed, preferred_element_type=jnp.float32).astype(
        jnp.bfloat16
    )
    outgoing = jnp.broadcast_to(packed[None], (2,) + packed.shape).reshape(
        ranks, -1, packed.shape[-1]
    )
    incoming = lax.all_to_all(outgoing, "dp", split_axis=0, concat_axis=0, tiled=True)
    local_count = w_gate.shape[0]
    arrived = incoming.reshape(ranks, local_count, STEPS * CAPACITY, D)
    gate = jnp.einsum("nlrd,ldf->nlrf", arrived, w_gate, preferred_element_type=jnp.float32)
    upper = jnp.einsum("nlrd,ldf->nlrf", arrived, w_up, preferred_element_type=jnp.float32)
    hidden_part = (jax.nn.silu(gate) * upper).astype(jnp.bfloat16)
    hidden_all = lax.all_gather(hidden_part, "rep", axis=3, tiled=True)
    produced = jnp.einsum(
        "nlrf,lfd->nlrd", hidden_all, w_down, preferred_element_type=jnp.float32
    ).astype(jnp.bfloat16)
    returned = lax.all_to_all(
        produced.reshape(ranks, -1, produced.shape[-1]),
        "dp",
        split_axis=0,
        concat_axis=0,
        tiled=True,
    )
    returned = returned.reshape(2, EXPERTS, STEPS, CAPACITY, -1).astype(jnp.float32)
    both_halves = returned[0] + returned[1]
    section_index = jnp.broadcast_to(
        jnp.arange(STEPS, dtype=jnp.int32)[:, None, None], route_ids.shape
    )
    picked = both_halves[route_ids, section_index, slots]
    weights = jax.nn.softmax(route_logits, axis=-1)
    moe_out = jnp.sum(weights[..., None] * picked, axis=2).astype(jnp.bfloat16)
    return (attn_out, moe_out)


def solution(mesh):
    return jax.shard_map(
        local,
        mesh=mesh,
        in_specs=(
            P(None, "dp", "rep"),
            P(None, "dp", "rep"),
            P(None, "dp", "rep"),
            P(),
            P(),
            P("dp", None, None, "rep"),
            P("dp", None),
            P("dp"),
            P("dp"),
            P("dp"),
            P(None, "dp", "rep"),
            P(),
            P(None, "dp", None),
            P(None, "dp", None),
            P("dp", None, "rep"),
            P("dp", None, "rep"),
            P("dp", None, "rep"),
        ),
        out_specs=(P(None, "dp", "rep"), P(None, "dp", "rep")),
        check_vma=False,
    )
```

profile of v0, /device:TPU:0, one launch (start us, length us, event | category | flops | bytes accessed | tf_op | source)
XLA Modules:
  0.0 276.7 jit_solution(1941087963766147365)
XLA Ops:
  0.7 1.4 copy.73
  3.2 7.9 %all_gather.6 = bf16[3,12,4096]{2,1,0:T(8,128)(2,1)S(1)} all-gather(bf16[3,12,1024]{2,1,0:T(8,128)(2,1)S(1)} %copy-done.4), channel_id=1, replica_groups=mesh['dp'=8,'rep'=4] {'rep'}, dimensions={2}, use_global_device_ids=true | all-gather | bytes 368640 | tf_op jit(solution)/shard_map/all_gather | solution.py:119
  11.3 1.0 fusion.10
  12.4 3.3 %copy.56 = bf16[64,3,2,4096]{3,2,1,0:T(2,128)(2,1)S(1)} copy(bf16[64,3,2,4096]{3,0,2,1:T(8,128)(2,1)S(1)} %fusion.10) | data formatting | bytes 6291456 | tf_op jit(solution)/shard_map/convert_element_type | solution.py:128
  15.7 6.7 %broadcast_in_dim.100 = bf16[2,64,3,2,4096]{4,3,2,1,0:T(2,128)(2,1)} broadcast(bf16[64,3,2,4096]{3,2,1,0:T(2,128)(2,1)S(1)} %copy.56), dimensions={1,2,3,4} | broadcast | bytes 9437184 | tf_op jit(solution)/shard_map/broadcast_in_dim | solution.py:131
  22.3 10.2 %reshape.979 = bf16[8,96,4096]{2,1,0:T(8,128)(2,1)} reshape(bf16[2,64,3,2,4096]{4,3,2,1,0:T(2,128)(2,1)} %broadcast_in_dim.100) | data formatting | bytes 12582912 | tf_op jit(solution)/shard_map/reshape | solution.py:131
  32.5 6.0 %all-to-all-start = ((bf16[8,96,4096]{2,1,0:T(8,128)(2,1)}), bf16[8,96,4096]{2,1,0:T(8,128)(2,1)}, u32[]{:S(2)}, u32[]{:S(2)}) async-start(bf16[8,96,4096]{2,1,0:T(8,128)(2,1)} %reshape.979), calls=%async_computation | async-start | bytes 12582912 | tf_op jit(solution)/shard_map/all_to_all | solution.py:134
  38.6 1.1 gather_fusion
  39.7 3.0 %collective-permute-start = (bf16[8,64,2,128]{3,2,1,0:T(2,128)(2,1)S(1)}, bf16[8,64,2,128]{3,2,1,0:T(2,128)(2,1)S(1)}, u32[]{:S(2)}, u32[]{:S(2)}) collective-permute-start(bf16[8,64,2,128]{3,2,1,0:T(2,128)(2,1)S(1)} %gather_fusion), channel_id=1, source_target_pairs={{0,16},{4,20},{8,24},{12,28},{16,0},{20,4},{24,8},{28,12},{1,17},{... | collective-permute-start | bytes 786440 | tf_op jit(solution)/shard_map/ppermute | solution.py:21
  44.9 138.8 %all-to-all-done = bf16[8,96,4096]{2,1,0:T(8,128)(2,1)} async-done(((bf16[8,96,4096]{2,1,0:T(8,128)(2,1)}), bf16[8,96,4096]{2,1,0:T(8,128)(2,1)}, u32[]{:S(2)}, u32[]{:S(2)}) %all-to-all-start) | async-done | bytes 6291488 | tf_op jit(solution)/shard_map/all_to_all | solution.py:134
  183.7 6.2 %copy.57 = bf16[8,96,4096]{2,0,1:T(8,128)(2,1)S(1)} copy(bf16[8,96,4096]{2,1,0:T(8,128)(2,1)} %all-to-all-done) | data formatting | bytes 12582912 | tf_op jit(solution)/shard_map/all_to_all | solution.py:134
  189.9 7.2 %fusion.14 = f32[8,16,6,128]{3,0,2,1:T(8,128)S(1)} fusion(bf16[8,16,6,4096]{3,0,2,1:T(8,128)(2,1)S(1)} %bitcast.116, bf16[16,4096,128]{2,1,0:T(8,128)(2,1)} %param.31), kind=kOutput, calls=%fused_computation.21 | convolution fusion | flops 805306368 | bytes 23461888 | tf_op jit(solution)/shard_map/nlrd,ldf->nlrf/dot_general | solution.py:137
  197.2 7.3 %fusion.35 = bf16[8,16,6,128]{3,0,2,1:T(8,128)(2,1)S(1)} fusion(bf16[8,16,6,4096]{3,0,2,1:T(8,128)(2,1)S(1)} %bitcast.117, bf16[16,4096,128]{2,1,0:T(8,128)(2,1)} %param.32, f32[8,16,6,128]{3,0,2,1:T(8,128)S(1)} %fusion.14), kind=kOutput, calls=%fused_computation.40 | convolution fusion | flops 805896192 | bytes 23658496 | tf_op jit(solution)/shard_map/nlrd,ldf->nlrf/dot_general | solution.py:138
  204.5 8.3 %all_gather.7 = bf16[8,16,6,512]{3,0,2,1:T(8,128)(2,1)S(1)} all-gather(bf16[8,16,6,128]{3,0,2,1:T(8,128)(2,1)S(1)} %fusion.35), channel_id=1, replica_groups=mesh['dp'=8,'rep'=4] {'rep'}, dimensions={3}, use_global_device_ids=true | all-gather | bytes 983040 | tf_op jit(solution)/shard_map/all_gather | solution.py:140
  212.8 8.8 %fusion.11 = bf16[16,8,6,1024]{3,1,2,0:T(8,128)(2,1)S(1)} fusion(bf16[8,16,6,512]{3,0,2,1:T(8,128)(2,1)S(1)} %all_gather.7, bf16[16,512,1024]{2,1,0:T(8,128)(2,1)} %param.33), kind=kOutput, calls=%fused_computation.16 | convolution fusion | flops 806092800 | bytes 19136512 | tf_op jit(solution)/shard_map/nlrf,lfd->nlrd/dot_general | solution.py:141
  221.6 2.0 copy.58
  223.6 4.5 %all-to-all-start.1 = ((bf16[8,96,1024]{2,1,0:T(8,128)(2,1)}), bf16[8,96,1024]{2,1,0:T(8,128)(2,1)}, u32[]{:S(2)}, u32[]{:S(2)}) async-start(bf16[8,96,1024]{2,1,0:T(8,128)(2,1)} %copy.58), calls=%async_computation.1 | async-start | bytes 3145728 | tf_op jit(solution)/shard_map/all_to_all | solution.py:144
  228.4 0.9 scatter_fusion
  229.3 6.1 %gather_fusion.1 = bf16[48,64,2,128]{3,2,1,0:T(2,128)(2,1)S(1)} fusion(bf16[48,64,2,128]{3,2,1,0:T(2,128)(2,1)S(1)} %scatter_fusion, s32[1024]{0:T(1024)S(1)} %pad_clamp_fusion), kind=kCustom, calls=%fused_computation.1 | custom fusion | bytes 3145920 | tf_op jit(solution)/shard_map/gather | solution.py:115
  235.5 0.4 copy.50
  235.9 1.7 broadcast_select_fusion
  237.6 1.1 copy-done
  239.1 0.7 copy-done.2
  240.0 1.7 convolution_convert_fusion.1
  242.2 0.7 copy-done.3
  243.1 1.4 convolution_convert_fusion.2
  245.6 0.7 pad_maximum_fusion
  246.3 19.4 %all-to-all-done.1 = bf16[8,96,1024]{2,1,0:T(8,128)(2,1)} async-done(((bf16[8,96,1024]{2,1,0:T(8,128)(2,1)}), bf16[8,96,1024]{2,1,0:T(8,128)(2,1)}, u32[]{:S(2)}, u32[]{:S(2)}) %all-to-all-start.1) | async-done | bytes 1572896 | tf_op jit(solution)/shard_map/all_to_all | solution.py:144
  265.7 1.8 convert_element_type.247
  267.7 0.9 add.151
  268.7 7.0 %gather_fusion.2 = f32[288,1024]{1,0:T(8,128)S(1)} fusion(f32[64,3,2,1024]{3,2,1,0:T(2,128)S(1)} %add.151, s32[288]{0:T(512)S(1)} %reshape.1005), kind=kCustom, calls=%fused_computation.2 | custom fusion | bytes 2362752 | tf_op jit(solution)/shard_map/gather | solution.py:156
  275.7 1.0 multiply_reduce_fusion
  (92 shorter events, 6.1 us)
Async XLA Ops:
  0.6 2.6 copy-start.4
  0.6 1.5 copy-start.8
  2.1 9.2 %copy-start.6 = (f32[4096]{0:T(1024)S(1)}, f32[4096]{0:T(1024)}, u32[]{:S(2)}) copy-start(f32[4096]{0:T(1024)} %param.28) | copy-start | bytes 49156
  32.5 6.0 %copy-start.14 = (s32[8]{0:T(128)S(1)}, s32[8]{0:T(128)}, u32[]{:S(2)}) copy-start(s32[8]{0:T(128)} %param.25) | copy-start | bytes 100
  32.5 10.2 %copy-start.10 = (s32[12,4]{0,1:T(4,128)S(1)}, s32[12,4]{0,1:T(4,128)}, u32[]{:S(2)}) copy-start(s32[12,4]{0,1:T(4,128)} %param.23) | copy-start | bytes 580
  32.5 10.4 %copy-start.1 = (bf16[3,12,2048]{2,1,0:T(8,128)(2,1)S(1)}, bf16[3,12,2048]{2,1,0:T(8,128)(2,1)}, u32[]{:S(2)}) copy-start(bf16[3,12,2048]{2,1,0:T(8,128)(2,1)} %param.17) | copy-start | bytes 442372
  32.5 151.2 %all-to-all-start = ((bf16[8,96,4096]{2,1,0:T(8,128)(2,1)}), bf16[8,96,4096]{2,1,0:T(8,128)(2,1)}, u32[]{:S(2)}, u32[]{:S(2)}) async-start(bf16[8,96,4096]{2,1,0:T(8,128)(2,1)} %reshape.979), calls=%async_computation | async-start | bytes 12582912 | tf_op jit(solution)/shard_map/all_to_all | solution.py:134
  38.5 4.6 %copy-start.5 = (bf16[3,12,128]{2,1,0:T(8,128)(2,1)S(1)}, bf16[3,12,128]{2,1,0:T(8,128)(2,1)}, u32[]{:S(2)}) copy-start(bf16[3,12,128]{2,1,0:T(8,128)(2,1)} %param.18) | copy-start | bytes 27652
  38.5 4.8 %copy-start.11 = (s32[12]{0:T(128)S(1)}, s32[12]{0:T(128)}, u32[]{:S(2)}) copy-start(s32[12]{0:T(128)} %param.24) | copy-start | bytes 148
  38.5 4.8 %copy-start.7 = (bf16[3,12,128]{2,1,0:T(8,128)(2,1)S(1)}, bf16[3,12,128]{2,1,0:T(8,128)(2,1)}, u32[]{:S(2)}) copy-start(bf16[3,12,128]{2,1,0:T(8,128)(2,1)} %param.19) | copy-start | bytes 27652
  38.5 4.8 %copy-start.12 = (f32[128]{0:T(128)S(1)}, f32[128]{0:T(128)}, u32[]{:S(2)}) copy-start(f32[128]{0:T(128)} %param.21) | copy-start | bytes 1540
  38.5 5.5 %copy-start.15 = (s32[8]{0:T(128)S(1)}, s32[8]{0:T(128)}, u32[]{:S(2)}) copy-start(s32[8]{0:T(128)} %param.26) | copy-start | bytes 100
  38.5 5.7 %copy-start.9 = (f32[3,12,8]{1,2,0:T(8,128)S(1)}, f32[3,12,8]{1,2,0:T(8,128)}, u32[]{:S(2)}) copy-start(f32[3,12,8]{1,2,0:T(8,128)} %param.30) | copy-start | bytes 3460
  38.6 6.1 %copy-start.13 = (f32[128]{0:T(128)S(1)}, f32[128]{0:T(128)}, u32[]{:S(2)}) copy-start(f32[128]{0:T(128)} %param.20) | copy-start | bytes 1540
  39.7 188.8 %collective-permute-start = (bf16[8,64,2,128]{3,2,1,0:T(2,128)(2,1)S(1)}, bf16[8,64,2,128]{3,2,1,0:T(2,128)(2,1)S(1)}, u32[]{:S(2)}, u32[]{:S(2)}) collective-permute-start(bf16[8,64,2,128]{3,2,1,0:T(2,128)(2,1)S(1)} %gather_fusion), channel_id=1, source_target_pairs={{0,16},{4,20},{8,24},{12,28},{16,0},{20,4},{24,8},{28,12},{1,17},{... | collective-permute-start | bytes 786440 | tf_op jit(solution)/shard_map/ppermute | solution.py:21
  223.6 42.1 %all-to-all-start.1 = ((bf16[8,96,1024]{2,1,0:T(8,128)(2,1)}), bf16[8,96,1024]{2,1,0:T(8,128)(2,1)}, u32[]{:S(2)}, u32[]{:S(2)}) async-start(bf16[8,96,1024]{2,1,0:T(8,128)(2,1)} %copy.58), calls=%async_computation.1 | async-start | bytes 3145728 | tf_op jit(solution)/shard_map/all_to_all | solution.py:144
  237.6 1.1 copy-start
  239.1 0.7 copy-start.2
  242.2 0.7 copy-start.3
where the time goes:
time: 277 us
  waiting for transfers between devices  158 us (57%)
  local copies, waits for them, and re-layouts  50 us (18%)
  matrix products  28.9 us (10%)
  blocking collectives  16.2 us (6%)
  starting transfers between devices  13.5 us (5%)
  other arithmetic  8.71 us (3%)
    all_to_all x1, waiting for transfers between devices, local(): lax.all_to_all(outgoing, 'dp', split_axis=0, concat_axis=0, tiled=True)  139 us
    all_to_all x1, waiting for transfers between devices, local(): lax.all_to_all(produced.reshape(ranks, -1, produced.shape[-1]), 'dp', spl...  19.4 us
    reshape x1, local copies, waits for them, and re-layouts, local(): jnp.broadcast_to(packed[None], (2,) + packed.shape)  10.2 us
    dot_general x1, matrix products, local(): jnp.einsum('nlrf,lfd->nlrd', hidden_all, w_down, preferred_element_type=j...  8.76 us
    all_gather x1, blocking collectives, local(): hidden_all = lax.all_gather(hidden_part, 'rep', axis=3, tiled=True)  8.3 us
    all_gather x1, blocking collectives, local(): whole_rows = lax.all_gather(hidden_in, 'rep', axis=2, tiled=True)  7.91 us
    dot_general x1, matrix products, local(): jnp.einsum('nlrd,ldf->nlrf', arrived, w_up, preferred_element_type=jnp.fl...  7.33 us
    dot_general x1, matrix products, local(): jnp.einsum('nlrd,ldf->nlrf', arrived, w_gate, preferred_element_type=jnp....  7.2 us
  transfers between devices with their start and end apart: 3, of which 2 were waited for; matrix products, arithmetic and copies ran while one was open for 18% of the time, Pallas kernels for 0%

commit v1 on v0

v1 whole, which is shorter than its diff:
```python
import functools
import math

import jax
import jax.numpy as jnp
import numpy as np
from jax import lax
from jax.experimental import pallas as pl
from jax.experimental.pallas import tpu as pltpu
from jax.sharding import PartitionSpec as P

D = 4096
HEAD_DIM = 128
EXPERTS = 64
STEPS = 3
CAPACITY = 2
TOP_K = 8
SLAB = 16
LANES = 128
PIECES = LANES // SLAB

EPS = 1e-06
THETA = 1000000.0

BF16 = jnp.bfloat16
F32 = jnp.float32
ANY = pl.BlockSpec(memory_space=pl.ANY)
VMEM = pl.BlockSpec(memory_space=pltpu.VMEM)
SMEM = pl.BlockSpec(memory_space=pltpu.SMEM)


def place(route_ids):
    flat_ids = route_ids.reshape(route_ids.shape[0], -1)
    hot_table = (
        flat_ids[:, :, None] == jnp.arange(EXPERTS, dtype=jnp.int32)[None, None, :]
    ).astype(jnp.int32)
    before = jnp.cumsum(hot_table, axis=1) - hot_table
    return jnp.sum(before * hot_table, axis=2).reshape(route_ids.shape)


def attention_kernel(
    first, count, table, lengths, slots_in, q_ref, k_ref, v_ref, qg_ref, kg_ref, speed_ref, pool_ref, new_ref, *refs
):
    out_ref, source, angles = refs[-3:]
    pool_count = pool_ref.shape[0]
    new_count = new_ref.shape[0]
    row_count = q_ref.shape[1]
    page_count = table.shape[0]
    page_rows = pool_ref.shape[1]
    heads = q_ref.shape[2] // HEAD_DIM
    if first:
        out_ref[...] = refs[0][...]
    for slot in range(pool_count):
        source[slot] = -1
    for at in range(new_count):
        source[slots_in[at]] = at

    def page_of(slot):
        at = source[slot]
        return jnp.where(at >= 0, new_ref[jnp.maximum(at, 0)], pool_ref[slot])

    scaling = 1.0 / math.sqrt(HEAD_DIM)
    angles[...] = jnp.zeros(angles.shape, F32)
    for step in range(STEPS):
        for row in range(row_count):
            position = (lengths[row] + step).astype(F32)
            angles[pl.ds(step * row_count + row, 1), :] = speed_ref[...] * position
    first_half = lax.broadcasted_iota(jnp.int32, angles.shape, 1) < HEAD_DIM // 2
    cosines = jnp.cos(angles[...])
    sines = jnp.sin(angles[...])
    sines = jnp.where(first_half, -sines, sines)

    def turned(values, gain, cosine, sine):
        mean_square = jnp.mean(values * values, axis=-1, keepdims=True)
        normed = values * lax.rsqrt(mean_square + EPS) * gain
        return (normed * cosine + pltpu.roll(normed, HEAD_DIM // 2, 1) * sine).astype(BF16)

    width = page_count * page_rows
    column = lax.broadcasted_iota(jnp.int32, (STEPS * heads, width), 1)
    fresh_column = lax.broadcasted_iota(jnp.int32, (STEPS * heads, STEPS), 1)
    fresh_row = lax.broadcasted_iota(jnp.int32, (STEPS * heads, STEPS), 0) // heads
    for row in range(first, first + count):
        queries = []
        keys = []
        for step in range(STEPS):
            at = step * row_count + row
            cosine = cosines[at : at + 1]
            sine = sines[at : at + 1]
            raw = q_ref[step, pl.ds(row, 1), :].astype(F32)
            raw = jnp.concatenate(
                [raw[:, h * HEAD_DIM : (h + 1) * HEAD_DIM] for h in range(heads)], axis=0
            )
            queries.append(turned(raw, qg_ref[...], cosine, sine))
            keys.append(turned(k_ref[step, pl.ds(row, 1), :].astype(F32), kg_ref[...], cosine, sine))
        queries = jnp.concatenate(queries, axis=0)
        context = jnp.concatenate(
            [page_of(table[page, row]) for page in range(page_count)], axis=0
        )
        contract = (((1,), (1,)), ((), ()))
        scores = lax.dot_general(queries, context, contract, preferred_element_type=F32) * scaling
        valid = (column < 2 * lengths[row]) & (column % 2 == 0)
        scores = jnp.where(valid, scores, -1e30)
        fresh = jnp.concatenate(
            [
                jnp.sum(queries.astype(F32) * key.astype(F32), axis=-1, keepdims=True)
                for key in keys
            ],
            axis=1,
        )
        fresh = jnp.where(fresh_column <= fresh_row, fresh * scaling, -1e30)
        top = jnp.maximum(
            jnp.max(scores, axis=-1, keepdims=True), jnp.max(fresh, axis=-1, keepdims=True)
        )
        expos = jnp.where(valid, jnp.exp(scores - top), 0.0)
        fresh = jnp.where(fresh_column <= fresh_row, jnp.exp(fresh - top), 0.0)
        total = jnp.sum(expos, axis=-1, keepdims=True) + jnp.sum(fresh, axis=-1, keepdims=True)
        probs = pltpu.roll(expos / total, 1, 1).astype(BF16)
        mixed = jnp.dot(probs, context, preferred_element_type=F32)
        fresh = (fresh / total).astype(BF16).astype(F32)
        for step in range(STEPS):
            value = v_ref[step, pl.ds(row, 1), :].astype(F32)
            mixed = mixed + fresh[:, step : step + 1] * value
        for step in range(STEPS):
            part = mixed[step * heads : (step + 1) * heads]
            out_ref[step, pl.ds(row, 1), :] = jnp.concatenate(
                [part[h : h + 1] for h in range(heads)], axis=1
            ).astype(BF16)


def attention(
    arriving, q_raw, k_raw, v_raw, q_gain, k_gain, pool, page_table, cache_len, in_slots, first, count,
    so_far=None, tie=None
):
    extra = [x for x in (so_far, tie) if x is not None]
    row_count = q_raw.shape[1]
    exponent = np.arange(HEAD_DIM // 2, dtype=np.float32) * np.float32(2.0 / HEAD_DIM)
    speed = np.power(np.float32(THETA), -exponent)
    speed = jnp.asarray(np.concatenate([speed, speed])[None], F32)
    scratch = [
        pltpu.SMEM((pool.shape[0],), jnp.int32),
        pltpu.VMEM((-(-STEPS * row_count // 8) * 8, HEAD_DIM), F32),
    ]
    return pl.pallas_call(
        functools.partial(attention_kernel, first, count),
        out_shape=jax.ShapeDtypeStruct(q_raw.shape, BF16),
        in_specs=[SMEM] * 3 + [VMEM] * (8 + (so_far is not None)) + [ANY] * (tie is not None),
        out_specs=VMEM,
        scratch_shapes=scratch,
        compiler_params=pltpu.CompilerParams(vmem_limit_bytes=12 << 20),
        cost_estimate=pl.CostEstimate(
            flops=400_000_000, bytes_accessed=8_000_000, transcendentals=400_000
        ),
        name="attention",
    )(
        page_table.T, cache_len, in_slots, q_raw, k_raw, v_raw, q_gain[None], k_gain[None], speed,
        pool, arriving, *extra,
    )


def swap(x, axis, bits):
    size = lax.axis_size(axis)
    return lax.ppermute(x, axis, [(i, i ^ bits) for i in range(size)])


def in_hbm(x):
    return pltpu.with_memory_space_constraint(x, pltpu.HBM)


def block_kernel(
    here, out_pages, ids_hbm, logits_hbm, hidden_hbm, gain_hbm, pool_ref, out_ref, leaving, ids_ref,
    logits_ref, hidden_ref, gain_ref, page_ids, wide, sems, page_sems,
):
    rank = here[0]
    row_count = ids_ref.shape[2]
    width = out_ref.shape[1]
    part = pl.ds(pl.multiple_of(here[1] * width, width), width)
    copies = [
        pltpu.make_async_copy(source, target, sems.at[at])
        for at, (source, target) in enumerate(
            (
                (ids_hbm, ids_ref),
                (logits_hbm, logits_ref),
                (hidden_hbm, hidden_ref),
                (gain_hbm.at[:, part], gain_ref),
                (out_pages, page_ids),
            )
        )
    ]
    for copy in copies:
        copy.start()
    lane_at = lax.broadcasted_iota(jnp.int32, (TOP_K, LANES), 1)
    wide[...] = jnp.zeros(wide.shape, F32)
    copies[4].wait()
    pages = [
        pltpu.make_async_copy(pool_ref.at[page_ids[at]], leaving.at[at], page_sems.at[at])
        for at in range(leaving.shape[0])
    ]
    for copy in pages:
        copy.start()
    copies[0].wait()
    copies[1].wait()
    groups = [jnp.zeros((4, LANES), F32) for _ in range(4)]

    def put(piece, value):
        turned = pltpu.roll(value, ((piece + rank) % PIECES) * SLAB, 1)
        groups[piece // PIECES] += turned

    for step in range(STEPS):
        wide[step, 0, :, :row_count] = ids_ref[step].astype(F32)
        wide[step, 1, :, :row_count] = logits_ref[step]
        ids = wide[step, 0]
        logits = wide[step, 1]
        expos = jnp.exp(logits - jnp.max(logits, axis=0, keepdims=True))
        weights = expos / jnp.sum(expos, axis=0, keepdims=True)
        high = weights.astype(BF16).astype(F32)
        slot = jnp.zeros((TOP_K, LANES), F32)
        for back in range(1, row_count):
            earlier = pltpu.roll(ids, back, 1)
            for k in range(TOP_K):
                same = (ids == earlier[k : k + 1]) & (lane_at >= back)
                slot = slot + jnp.where(same, 1.0, 0.0)
        for at, value in enumerate((ids * CAPACITY + slot + 1.0, high, weights - high)):
            value = jnp.where(lane_at < row_count, value, 0.0)
            for side in range(2):
                put((2 * step + side) * 3 + at, value[4 * side : 4 * side + 4])
    copies[2].wait()
    copies[3].wait()
    gain = gain_ref[...]
    row_at = lax.broadcasted_iota(jnp.int32, (row_count, LANES), 0)
    column_at = lax.broadcasted_iota(jnp.int32, (row_count, LANES), 1)
    rows = []
    for step in range(STEPS):
        values = hidden_ref[step].astype(F32)
        square = jnp.sum(values * values, axis=-1, keepdims=True)
        rest = jnp.sum(jnp.where(row_at == column_at, square, 0.0), axis=0, keepdims=True)
        rest = jnp.concatenate([rest, jnp.zeros((3, LANES), F32)], axis=0)
        for at in range(3):
            high = rest.astype(BF16).astype(F32)
            put(18 + 3 * step + at, high)
            rest = rest - high
        rows.append(values * gain)
    groups.append(jnp.zeros((4, width - 4 * LANES), F32))
    out_ref[...] = jnp.concatenate(rows + [jnp.concatenate(groups, axis=1)], axis=0).astype(BF16)
    for copy in pages:
        copy.wait()


def line_kernel(b0, b1, b2, b3, line_ref):
    for at, block in enumerate((b0, b1, b2, b3)):
        line_ref[at] = block[...]


def relay_kernel(*refs):
    *parts, _, out_ref = refs
    at = 0
    for part in parts:
        out_ref[at : at + part.shape[0]] = part[...]
        at += part.shape[0]


def relay(*parts, tie):
    length = sum(part.shape[0] for part in parts)
    return pl.pallas_call(
        relay_kernel,
        out_shape=jax.ShapeDtypeStruct((length,) + parts[0].shape[1:], parts[0].dtype),
        in_specs=[VMEM] * len(parts) + [ANY],
        out_specs=VMEM,
        compiler_params=pltpu.CompilerParams(vmem_limit_bytes=4 << 20),
        name="relay",
    )(*parts, tie)


def by_groups(count, group, copies, work):
    group = math.gcd(count, group)

    @pl.loop(0, count // group)
    def _(at):
        experts = [at * group + e for e in range(group)]
        for e in experts:
            for copy in copies(e):
                copy.wait()
        work(experts)


def up_kernel(pieces, here, *refs):
    first, last = pieces[0] == 0, pieces[-1] == 3
    count = len(pieces)
    if not first:
        line = refs[0].shape[0] // 2
        blocks = [ref.at[pl.ds(at, line)] for ref in refs[:count] for at in (0, line)]
        refs = refs[count:]
    else:
        blocks, refs = refs[: 2 * count], refs[2 * count :]
    wg_ref, wu_ref = refs[:2]
    refs = refs[2:]
    if first:
        gate_ref, upper_ref, square_ref, hot_ref, share_ref = refs[-10:-5]
        weights, rows, picked, info, sems = refs[-5:]
    elif last:
        gate_in, upper_in, square_in, hot_ref, share_ref = refs[:5]
        hid_ref, weights, rows, picked, info, sems, inverse = refs[-7:]
    else:
        gate_in, upper_in, square_in, hot_ref = refs[:4]
        gate_ref, upper_ref, square_ref, weights, rows, picked, info, sems = refs[-8:]
    line, tall, width = blocks[0].shape
    ranks = 2 * line
    shard_count, _, units = wg_ref.shape
    slab = ranks * CAPACITY
    picks = shard_count * slab
    lanes = ranks * SLAB
    rank, base = here[0], here[2]

    def copies(e):
        for at, piece in enumerate(pieces):
            source = pl.ds(pl.multiple_of((here[1] ^ piece) * width, width), width)
            target = pl.ds(at * width, width)
            for side, ref in enumerate((wg_ref, wu_ref)):
                yield pltpu.make_async_copy(
                    ref.at[e, source], weights.at[e, side, target], sems.at[2 * at + side, e]
                )

    @pl.loop(0, shard_count)
    def _(e):
        for copy in copies(e):
            copy.start()

    @pl.loop(0, line)
    def _(m):
        for at, ref in enumerate(blocks):
            at, side = at // 2, at % 2
            dp = rank ^ (2 * m + side)
            to = pl.ds(pl.multiple_of(dp * SLAB, SLAB), SLAB)
            values = ref[m].astype(F32)
            for step in range(STEPS):
                rows[step, to, pl.ds(at * width, width)] = values[
                    step * 12 : step * 12 + SLAB
                ].astype(BF16)
            info[at, dp] = values[tall - 8 :, : 4 * LANES]

    slot_at = lax.broadcasted_iota(jnp.int32, (4, lanes), 1) // SLAB

    def line_of(at, number):
        group = pl.ds(number // PIECES * LANES, LANES)
        found = jnp.zeros((4, lanes), F32)
        for d in range(ranks):
            found += jnp.where(slot_at == (number + d) % PIECES, info[at, d, 4:, group], 0.0)
        back = number % PIECES * SLAB
        return pltpu.roll(found, lanes - back, 1) if back else found

    squares = []
    for step in range(STEPS):
        total = sum(line_of(at, 18 + 3 * step + part) for at in range(count) for part in range(3))
        squares.append(total[:1] if first else total[:1] + square_in[step : step + 1])
        if not last:
            square_ref[pl.ds(step, 1), :] = squares[step]
    if first:
        row_at = lax.broadcasted_iota(jnp.int32, (picks, lanes), 0)
        lane_at = lax.broadcasted_iota(jnp.int32, (picks, lanes), 1)
        owner = (row_at % slab) // CAPACITY
        wanted = (base + row_at // slab) * CAPACITY + row_at % CAPACITY + 1
        wanted = jnp.where(lane_at // SLAB == owner, wanted, -1).astype(F32)
        for step in range(STEPS):
            hot = jnp.zeros((picks, lanes), F32)
            gate = jnp.zeros((picks, lanes), F32)
            for side in range(2):
                number = (2 * step + side) * 3
                marks = line_of(0, number)
                share = line_of(0, number + 1) + line_of(0, number + 2)
                for k in range(4):
                    found = marks[k : k + 1] == wanted
                    hot = jnp.where(found, 1.0, hot)
                    gate = jnp.where(found, share[k : k + 1], gate)
            hot_ref[step] = hot.astype(BF16)
            gate = jnp.broadcast_to(jnp.sum(gate, axis=-1, keepdims=True), (picks, units))
            share_ref[:, pl.ds(step * slab, slab), :] = gate.reshape(shard_count, slab, units)

    for step in range(STEPS):
        hot = hot_ref[step]
        for n in range(0, count * width, 256):
            for half in range(0, picks, picks // 2):
                chosen = jnp.dot(
                    hot[half : half + picks // 2],
                    rows[step, :, n : n + 256],
                    preferred_element_type=F32,
                ).astype(BF16)
                picked[
                    pl.ds(half // slab, shard_count // 2), pl.ds(step * slab, slab), pl.ds(n, 256)
                ] = chosen.reshape(shard_count // 2, slab, 256)
        if last:
            found = hot.astype(F32) * lax.rsqrt(squares[step] / D + EPS)
            found = jnp.broadcast_to(jnp.sum(found, axis=-1, keepdims=True), (picks, units))
            inverse[:, pl.ds(step * slab, slab), :] = found.reshape(shard_count, slab, units)

    def multiply(experts):
        gates = [jnp.dot(picked[e], weights[e, 0], preferred_element_type=F32) for e in experts]
        uppers = [jnp.dot(picked[e], weights[e, 1], preferred_element_type=F32) for e in experts]
        for e, gate, upper in zip(experts, gates, uppers):
            if not first:
                gate = gate + gate_in[e]
                upper = upper + upper_in[e]
            if last:
                gate = gate * inverse[e]
                upper = upper * inverse[e]
                hid_ref[e] = (gate * jax.nn.sigmoid(gate) * upper * share_ref[e]).astype(BF16)
            else:
                gate_ref[e] = gate
                upper_ref[e] = upper

    by_groups(shard_count, 2, copies, multiply)


def up_pieces(pieces, here, blocks, w_gate, w_up, so_far=(), ties=()):
    width = blocks[0].shape[2]
    shard_count, _, units = w_gate.shape
    ranks = lax.axis_size("dp")
    slab = ranks * CAPACITY
    depth = len(pieces) * width
    product = jax.ShapeDtypeStruct((shard_count, STEPS * slab, units), F32)
    hidden = jax.ShapeDtypeStruct(product.shape, BF16)
    square = jax.ShapeDtypeStruct((STEPS, LANES), F32)
    hot = jax.ShapeDtypeStruct((STEPS, shard_count * slab, ranks * SLAB), BF16)
    out = [product, product, square]
    if pieces[0] == 0:
        out += [hot, product]
    if pieces[-1] == 3:
        out = [hidden]
    scratch = [
        pltpu.VMEM((shard_count, 2, depth, units), BF16),
        pltpu.VMEM((STEPS, ranks * SLAB, depth), BF16),
        pltpu.VMEM((shard_count, STEPS * slab, depth), BF16),
        pltpu.VMEM((len(pieces), ranks, 8, 4 * LANES), F32),
        pltpu.SemaphoreType.DMA((2 * len(pieces), shard_count)),
    ]
    if pieces[-1] == 3:
        scratch.append(pltpu.VMEM(product.shape, F32))
    return pl.pallas_call(
        functools.partial(up_kernel, pieces),
        out_shape=out,
        in_specs=[SMEM] + [VMEM] * len(blocks) + [ANY] * 2 + [VMEM] * len(so_far) + [ANY] * len(ties),
        out_specs=[VMEM] * len(out),
        scratch_shapes=scratch,
        compiler_params=pltpu.CompilerParams(vmem_limit_bytes=32 << 20),
        cost_estimate=pl.CostEstimate(
            flops=1_000_000, bytes_accessed=len(pieces) * 100_000, transcendentals=1000
        ),
        name="gate_and_up",
    )(here, *blocks, w_gate, w_up, *so_far, *ties)


def down_kernel(piece, here, own_ref, other_ref, hot_ref, w_ref, *refs):
    weights, hidden, made, sums, sems = refs[-5:]
    if piece == 0:
        out_ref = refs[-6]
    else:
        out_ref, send_ref = refs[-7:-5]
    shard_count, _, units = own_ref.shape
    width = w_ref.shape[2]
    slab = made.shape[1] // shard_count
    rep = here[1]
    part = pl.ds(pl.multiple_of(((rep >> 1) ^ piece) * 2 * units, 2 * units), 2 * units)

    def copies(e):
        return [pltpu.make_async_copy(w_ref.at[e, part], weights.at[e], sems.at[e])]

    @pl.loop(0, shard_count)
    def _(e):
        copies(e)[0].start()

    for at, ref in enumerate((own_ref, other_ref)):
        at = ((rep & 1) ^ at) * units
        hidden[:, :, pl.ds(pl.multiple_of(at, units), units)] = ref[...]

    def multiply(experts):
        for e in experts:
            output = jnp.dot(hidden[e], weights[e], preferred_element_type=F32).astype(BF16)
            for step in range(STEPS):
                made[step, pl.ds(pl.multiple_of(e * slab, slab), slab), :] = output[
                    step * slab : (step + 1) * slab
                ]

    by_groups(shard_count, 4, copies, multiply)
    contract = (((0,), (0,)), ((), ()))
    for n in range(0, width, 256):
        at = slice(n, n + 256)
        for step in range(STEPS):
            total = lax.dot_general(
                hot_ref[step], made[step, :, at], contract, preferred_element_type=F32
            )
            if piece == 0:
                out_ref[step, :, at] = total
            else:
                sums[step, :, at] = refs[0][step, :, at] + total
    if piece == 1:
        for side, ref in enumerate((out_ref, send_ref)):
            for z in range(out_ref.shape[0]):
                at = pl.ds(pl.multiple_of((2 * z + ((here[0] & 1) ^ side)) * SLAB, SLAB), SLAB)
                ref[z] = jnp.concatenate(
                    [
                        sums[step, at, n : n + LANES][:12]
                        for step in range(STEPS)
                        for n in range(0, width, LANES)
                    ],
                    axis=0,
                ).astype(BF16)


def down_piece(piece, here, own, other, hot, w_down, so_far=(), ties=()):
    shard_count, _, width = w_down.shape
    _, picks, lanes = hot.shape
    units = own.shape[2]
    if piece == 0:
        out = [jax.ShapeDtypeStruct((STEPS, lanes, width), F32)]
    else:
        half = (lanes // SLAB // 2, STEPS * 12 * width // LANES, LANES)
        out = [jax.ShapeDtypeStruct(half, BF16)] * 2
    return pl.pallas_call(
        functools.partial(down_kernel, piece),
        out_shape=out,
        in_specs=[SMEM] + [VMEM] * 3 + [ANY] + [VMEM] * len(so_far) + [ANY] * len(ties),
        out_specs=[VMEM] * len(out),
        scratch_shapes=[
            pltpu.VMEM((shard_count, 2 * units, width), BF16),
            pltpu.VMEM((shard_count, own.shape[1], 2 * units), BF16),
            pltpu.VMEM((STEPS, picks, width), BF16),
            pltpu.VMEM((STEPS, lanes, width), F32),
            pltpu.SemaphoreType.DMA((shard_count,)),
        ],
        compiler_params=pltpu.CompilerParams(vmem_limit_bytes=24 << 20),
        cost_estimate=pl.CostEstimate(
            flops=1_000_000, bytes_accessed=100_000, transcendentals=0
        ),
        name="down",
    )(here, own, other, hot, w_down, *so_far, *ties)


def fold_kernel(here, keep_ref, got_ref, tie, own_ref, *send_refs):
    z = here[0] // 2
    own_ref[...] = keep_ref[z].astype(F32) + got_ref[z].astype(F32)
    for at, ref in enumerate(send_refs):
        to = z ^ (at + 1)
        ref[...] = (keep_ref[to].astype(F32) + got_ref[to].astype(F32)).astype(BF16)


def finish_kernel(own_ref, *refs):
    *parts, out_ref = refs
    total = own_ref[...]
    for part in parts:
        total = total + part[...].astype(F32)
    row_count = out_ref.shape[1]
    at = 0
    for step in range(STEPS):
        for n in range(0, out_ref.shape[2], LANES):
            out_ref[step, :, n : n + LANES] = total[at : at + row_count].astype(BF16)
            at += row_count


def gathered(
    q_raw, k_raw, v_raw, q_gain, k_gain, kv_pool, page_table, cache_len, out_pages, in_slots,
    hidden_in, ln_gain, route_ids, route_logits, w_gate, w_up, w_down,
):
    ranks = lax.axis_size("dp")
    shard_count = w_gate.shape[0]
    row_count = hidden_in.shape[1]
    width = hidden_in.shape[2]
    tall = STEPS * row_count + 4
    rank = lax.axis_index("dp").astype(jnp.int32)
    rep = lax.axis_index("rep").astype(jnp.int32)
    here = jnp.stack([rank, rep, rank * shard_count % EXPERTS])
    pool = kv_pool.reshape(kv_pool.shape[0], -1, kv_pool.shape[3])
    small = pltpu.CompilerParams(vmem_limit_bytes=4 << 20)
    ids = route_ids.transpose(0, 2, 1)
    logits = route_logits.transpose(0, 2, 1)
    block, leaving = pl.pallas_call(
        block_kernel,
        out_shape=(
            jax.ShapeDtypeStruct((tall, width), BF16),
            jax.ShapeDtypeStruct(out_pages.shape + pool.shape[1:], BF16),
        ),
        in_specs=[SMEM] + [ANY] * 6,
        out_specs=(VMEM, ANY),
        scratch_shapes=[
            pltpu.VMEM(ids.shape, jnp.int32),
            pltpu.VMEM(logits.shape, F32),
            pltpu.VMEM(hidden_in.shape, BF16),
            pltpu.VMEM((1, width), F32),
            pltpu.SMEM(out_pages.shape, jnp.int32),
            pltpu.VMEM((STEPS, 2, TOP_K, LANES), F32),
            pltpu.SemaphoreType.DMA((5,)),
            pltpu.SemaphoreType.DMA(out_pages.shape),
        ],
        compiler_params=small,
        name="token_block",
    )(
        here, in_hbm(out_pages), in_hbm(ids), in_hbm(logits), in_hbm(hidden_in), in_hbm(ln_gain[None]),
        in_hbm(pool),
    )
    w_gate, w_up, w_down = in_hbm(w_gate), in_hbm(w_up), in_hbm(w_down)
    own = pl.pallas_call(
        line_kernel,
        out_shape=jax.ShapeDtypeStruct((ranks // 2, tall, width), BF16),
        in_specs=[VMEM] * 4,
        out_specs=VMEM,
        compiler_params=small,
        name="line",
    )(block, *[swap(block, "dp", bits) for bits in (2, 4, 6)])
    other = swap(own, "dp", 1)
    far_own = swap(own, "rep", 2)
    near_own = swap(own, "rep", 1)
    arriving = lax.ppermute(leaving, "dp", [(i, (i + ranks // 2) % ranks) for i in range(ranks)])
    far_other = swap(other, "rep", 2)
    near_other = swap(other, "rep", 1)
    *sums, hot, share = up_pieces(
        (0, 1), here, (own, other, near_own, near_other), w_gate, w_up, ties=(far_own,)
    )
    far = relay(far_own, far_other, tie=sums[2])
    last = swap(far, "rep", 1)
    (hidden,) = up_pieces((2, 3), here, (far, last), w_gate, w_up, (*sums, hot, share))
    near = swap(hidden, "rep", 1)
    far = swap(hidden, "rep", 2)
    (sums,) = down_piece(0, here, hidden, near, hot, w_down, ties=(arriving,))
    far = relay(far, tie=sums)
    last = swap(far, "rep", 1)
    keep, send = down_piece(1, here, far, last, hot, w_down, (sums,))
    got = swap(send, "dp", 1)
    attend = functools.partial(
        attention, arriving, q_raw, k_raw, v_raw, q_gain, k_gain, pool, page_table, cache_len, in_slots
    )
    beside_y = row_count * 3 // 4
    attn_out = attend(0, beside_y, tie=keep)
    part = jax.ShapeDtypeStruct(keep.shape[1:], BF16)
    own, *sends = pl.pallas_call(
        fold_kernel,
        out_shape=[jax.ShapeDtypeStruct(part.shape, F32)] + [part] * 3,
        in_specs=[SMEM] + [VMEM] * 2 + [ANY],
        out_specs=[VMEM] * 4,
        compiler_params=small,
        name="fold",
    )(here, keep, got, attn_out)
    parts = [swap(send, "dp", 2 * at + 2) for at, send in enumerate(sends)]
    attn_out = attend(beside_y, row_count - beside_y, attn_out, tie=own)
    moe_out = pl.pallas_call(
        finish_kernel,
        out_shape=jax.ShapeDtypeStruct(hidden_in.shape, BF16),
        in_specs=[VMEM] * 4,
        out_specs=VMEM,
        compiler_params=small,
        name="finish",
    )(own, *parts)
    return attn_out, moe_out


def experts_exchanged(hidden_in, ln_gain, route_ids, route_logits, w_gate, w_up, w_down):
    ranks = lax.axis_size("dp")
    row_count = hidden_in.shape[1]
    whole_rows = lax.all_gather(hidden_in, "rep", axis=2, tiled=True)
    values = whole_rows.astype(F32)
    mean_square = jnp.mean(values * values, axis=-1, keepdims=True)
    normed = (values * lax.rsqrt(mean_square + EPS) * ln_gain).astype(BF16)
    slots = place(route_ids)
    targets = route_ids * CAPACITY + slots
    expert_slots = jnp.arange(EXPERTS * CAPACITY, dtype=jnp.int32)
    hits = jnp.any(targets[:, None, :, :] == expert_slots[None, :, None, None], axis=-1)
    hits = hits.astype(BF16).reshape(STEPS, EXPERTS, CAPACITY, row_count)
    packed = jnp.einsum("secr,srd->escd", hits, normed, preferred_element_type=F32).astype(BF16)
    outgoing = jnp.broadcast_to(packed[None], (2,) + packed.shape).reshape(
        ranks, -1, packed.shape[-1]
    )
    incoming = lax.all_to_all(outgoing, "dp", split_axis=0, concat_axis=0, tiled=True)
    local_count = w_gate.shape[0]
    arrived = incoming.reshape(ranks, local_count, STEPS * CAPACITY, D)
    gate = jnp.einsum("nlrd,ldf->nlrf", arrived, w_gate, preferred_element_type=F32)
    upper = jnp.einsum("nlrd,ldf->nlrf", arrived, w_up, preferred_element_type=F32)
    hidden_part = (jax.nn.silu(gate) * upper).astype(BF16)
    hidden_all = lax.all_gather(hidden_part, "rep", axis=3, tiled=True)
    produced = jnp.einsum("nlrf,lfd->nlrd", hidden_all, w_down, preferred_element_type=F32)
    produced = produced.astype(BF16)
    returned = lax.all_to_all(
        produced.reshape(ranks, -1, produced.shape[-1]), "dp", split_axis=0, concat_axis=0, tiled=True
    )
    returned = returned.reshape(2, EXPERTS, STEPS, CAPACITY, -1).astype(F32)
    both_halves = returned[0] + returned[1]
    section_index = jnp.broadcast_to(
        jnp.arange(STEPS, dtype=jnp.int32)[:, None, None], route_ids.shape
    )
    picked = both_halves[route_ids, section_index, slots]
    weights = jax.nn.softmax(route_logits, axis=-1)
    return jnp.sum(weights[..., None] * picked, axis=2).astype(BF16)


def exchanged(
    q_raw, k_raw, v_raw, q_gain, k_gain, kv_pool, page_table, cache_len, out_pages, in_slots,
    hidden_in, ln_gain, route_ids, route_logits, w_gate, w_up, w_down,
):
    ranks = lax.axis_size("dp")
    pool = kv_pool.reshape(kv_pool.shape[0], -1, kv_pool.shape[3])
    leaving = pool[out_pages]
    arriving = lax.ppermute(leaving, "dp", [(i, (i + ranks // 2) % ranks) for i in range(ranks)])
    attn_out = attention(
        arriving, q_raw, k_raw, v_raw, q_gain, k_gain, pool, page_table, cache_len, in_slots,
        0, q_raw.shape[1],
    )
    moe_out = experts_exchanged(hidden_in, ln_gain, route_ids, route_logits, w_gate, w_up, w_down)
    return attn_out, moe_out


def local(*args):
    plan = gathered if (lax.axis_size("dp"), lax.axis_size("rep")) == (8, 4) else exchanged
    return plan(*args)


def solution(mesh):
    return jax.shard_map(
        local,
        mesh=mesh,
        in_specs=(
            P(None, "dp", "rep"),
            P(None, "dp", "rep"),
            P(None, "dp", "rep"),
            P(),
            P(),
            P("dp", None, None, "rep"),
            P("dp", None),
            P("dp"),
            P("dp"),
            P("dp"),
            P(None, "dp", "rep"),
            P(),
            P(None, "dp", None),
            P(None, "dp", None),
            P("dp", None, "rep"),
            P("dp", None, "rep"),
            P("dp", None, "rep"),
        ),
        out_specs=(P(None, "dp", "rep"), P(None, "dp", "rep")),
        check_vma=False,
    )
```

time: 277 us -> 79.9 us (0.29)
  waiting for transfers between devices: 158 us -> 20.1 us
  local copies, waits for them, and re-layouts: 50 us -> 0.06 us
  Pallas kernels: 0 us -> 37.1 us
  matrix products: 28.9 us -> 0 us
  blocking collectives: 16.2 us -> 0 us
  other arithmetic: 8.71 us -> 0.08 us
  starting transfers between devices: 13.5 us -> 21.5 us
    all_to_all x2 -> x0, waiting for transfers between devices: 158 us -> none  [the longest x1 139 us: local(): lax.all_to_all(outgoing, 'dp', split_axis=0, concat_axis=0, tiled=True)]
    pallas_call x0 -> x12, Pallas kernels: none -> 37.1 us  [the longest x2 14.7 us: up_pieces(): pl.pallas_call(functools.partial(up_kernel, pieces), out_shape=out, in_sp...]
    dot_general x10 -> x0, matrix products: 28.9 us -> none  [the longest x1 8.76 us: local(): jnp.einsum('nlrf,lfd->nlrd', hidden_all, w_down, preferred_element_type=j...]
    ppermute x1 -> x17, waiting for transfers between devices: 0.01 us -> 20.1 us  [the longest x16 16.7 us: swap(): return lax.ppermute(x, axis, [(i, i ^ bits) for i in range(size)])]
    ppermute x1 -> x17, starting transfers between devices: 2.98 us -> 21.5 us  [the longest x16 18.2 us: swap(): return lax.ppermute(x, axis, [(i, i ^ bits) for i in range(size)])]
    all_gather x2 -> x0, blocking collectives: 16.2 us -> none  [the longest x1 8.3 us: local(): hidden_all = lax.all_gather(hidden_part, 'rep', axis=3, tiled=True)]
    gather x4 -> x0, local copies, waits for them, and re-layouts: 14.6 us -> none  [the longest x1 7 us: local(): picked = both_halves[route_ids, section_index, slots]]
    reshape x4 -> x0, local copies, waits for them, and re-layouts: 12.3 us -> none  [the longest x1 10.2 us: local(): jnp.broadcast_to(packed[None], (2,) + packed.shape)]
  transfers between devices with their start and end apart: 3 -> 17, of which waited for: 2 -> 8; matrix products, arithmetic and copies ran while one was open for 18% -> 0% of each run, Pallas kernels for 0% -> 35%
where the time goes in v1:
time: 79.9 us; the launch traced here: 79.7 us
  Pallas kernels  37.1 us (46%)
  starting transfers between devices  21.5 us (27%)
  waiting for transfers between devices  20.1 us (25%)
  between operations  0.89 us (1%)
    ppermute x16, starting transfers between devices, swap(): return lax.ppermute(x, axis, [(i, i ^ bits) for i in range(size)])  18.2 us
    ppermute x16, waiting for transfers between devices, swap(): return lax.ppermute(x, axis, [(i, i ^ bits) for i in range(size)])  16.7 us
    pallas_call x2, Pallas kernels, up_pieces(): pl.pallas_call(functools.partial(up_kernel, pieces), out_shape=out, in_sp...  14.7 us
    pallas_call x2, Pallas kernels, down_piece(): pl.pallas_call(functools.partial(down_kernel, piece), out_shape=out, in_s...  10.2 us
    pallas_call x2, Pallas kernels, attention(): pl.pallas_call(functools.partial(attention_kernel, first, count), out_sha...  8.53 us
    ppermute x1, waiting for transfers between devices, gathered(): lax.ppermute(leaving, 'dp', [(i, (i + ranks // 2) % ranks) for i in range...  3.33 us
    ppermute x1, starting transfers between devices, gathered(): lax.ppermute(leaving, 'dp', [(i, (i + ranks // 2) % ranks) for i in range...  3.28 us
    pallas_call x1, Pallas kernels, gathered(): pl.pallas_call(block_kernel, out_shape=(jax.ShapeDtypeStruct((tall, width...  2.34 us
  transfers between devices with their start and end apart: 17, of which 8 were waited for; matrix products, arithmetic and copies ran while one was open for 0% of the time, Pallas kernels for 35%

profile of v1, /device:TPU:0, one launch (start us, length us, event | category | flops | bytes accessed | tf_op | source)
XLA Modules:
  0.0 79.7 jit_solution(139128810708774004)
XLA Ops:
  0.6 0.1 pad_add_fusion.here
  0.7 2.3 %token_block.1 = (bf16[40,1024]{1,0:T(8,128)(2,1)S(1)}, bf16[8,128,128]{2,1,0:T(8,128)(2,1)S(1)}) custom-call(s32[3]{0:T(128)S(1)} %pad_add_fusion.here, s32[8]{0:T(128)} %out_pages.1, s32[3,8,12]{2,1,0:T(8,128)} %bitcast.20, f32[3,8,12]{2,1,0:T(8,128)} %bitcast.21, bf16[3,12,1024]{2,1,0:T(8,128)(2,1)} %hidden_hbm.1, f32[1,4096]{1,0:T(1,128)} %bitcast.19, ...), custom_call_target="tpu_custom_call" | custom-call | tf_op jit(solution)/shard_map/token_block/pallas_call | solution.py:573
  3.1 3.1 %collective-permute-start.1 = (bf16[40,1024]{1,0:T(8,128)(2,1)S(1)}, bf16[40,1024]{1,0:T(8,128)(2,1)S(1)}, u32[]{:S(2)}, u32[]{:S(2)}) collective-permute-start(bf16[40,1024]{1,0:T(8,128)(2,1)S(1)} %get-tuple-element.16.b0), channel_id=1, source_target_pairs={{0,8},{4,12},{8,0},{12,4},{16,24},{20,28},{24,16},{28,20},{1,9},{5... | collective-permute-start | bytes 245768 | tf_op jit(solution)/shard_map/ppermute | solution.py:162
  6.2 2.6 %collective-permute-start.2 = (bf16[40,1024]{1,0:T(8,128)(2,1)S(1)}, bf16[40,1024]{1,0:T(8,128)(2,1)S(1)}, u32[]{:S(2)}, u32[]{:S(2)}) collective-permute-start(bf16[40,1024]{1,0:T(8,128)(2,1)S(1)} %get-tuple-element.16.b0), channel_id=1, source_target_pairs={{0,16},{4,20},{8,24},{12,28},{16,0},{20,4},{24,8},{28,12},{1,17},{... | collective-permute-start | bytes 245768 | tf_op jit(solution)/shard_map/ppermute | solution.py:162
  8.8 6.6 %collective-permute-done.2.b2 = bf16[40,1024]{1,0:T(8,128)(2,1)S(1)} collective-permute-done((bf16[40,1024]{1,0:T(8,128)(2,1)S(1)}, bf16[40,1024]{1,0:T(8,128)(2,1)S(1)}, u32[]{:S(2)}, u32[]{:S(2)}) %collective-permute-start.2) | collective-permute-done | bytes 81952 | tf_op jit(solution)/shard_map/ppermute | solution.py:162
  15.4 1.6 %collective-permute-start.5 = (bf16[4,40,1024]{2,1,0:T(8,128)(2,1)S(1)}, bf16[4,40,1024]{2,1,0:T(8,128)(2,1)S(1)}, u32[]{:S(2)}, u32[]{:S(2)}) collective-permute-start(bf16[4,40,1024]{2,1,0:T(8,128)(2,1)S(1)} %line.1.refs_0_), channel_id=1, source_target_pairs={{0,4},{4,0},{8,12},{12,8},{16,20},{20,16},{24,28},{28,24},{1,5},{5... | collective-permute-start | bytes 983048 | tf_op jit(solution)/shard_map/ppermute | solution.py:162
  17.0 1.5 %collective-permute-start.4 = (bf16[4,40,1024]{2,1,0:T(8,128)(2,1)S(1)}, bf16[4,40,1024]{2,1,0:T(8,128)(2,1)S(1)}, u32[]{:S(2)}, u32[]{:S(2)}) collective-permute-start(bf16[4,40,1024]{2,1,0:T(8,128)(2,1)S(1)} %line.1.refs_0_), channel_id=1, source_target_pairs={{0,2},{1,3},{2,0},{3,1},{4,6},{5,7},{6,4},{7,5},{8,10},{9,11},{10,... | collective-permute-start | bytes 983048 | tf_op jit(solution)/shard_map/ppermute | solution.py:162
  18.5 4.5 %collective-permute-done.5.refs_1_ = bf16[4,40,1024]{2,1,0:T(8,128)(2,1)S(1)} collective-permute-done((bf16[4,40,1024]{2,1,0:T(8,128)(2,1)S(1)}, bf16[4,40,1024]{2,1,0:T(8,128)(2,1)S(1)}, u32[]{:S(2)}, u32[]{:S(2)}) %collective-permute-start.5) | collective-permute-done | bytes 327712 | tf_op jit(solution)/shard_map/ppermute | solution.py:162
  23.0 1.5 %collective-permute-start.6 = (bf16[4,40,1024]{2,1,0:T(8,128)(2,1)S(1)}, bf16[4,40,1024]{2,1,0:T(8,128)(2,1)S(1)}, u32[]{:S(2)}, u32[]{:S(2)}) collective-permute-start(bf16[4,40,1024]{2,1,0:T(8,128)(2,1)S(1)} %collective-permute-done.5.refs_1_), channel_id=1, source_target_pairs={{0,2},{1,3},{2,0},{3,1},{4,6},{5,7},{6,4},{7,5},{8,10},{9,11},{10,... | collective-permute-start | bytes 983048 | tf_op jit(solution)/shard_map/ppermute | solution.py:162
  24.5 0.1 collective-permute-done.8.refs_3_
  24.6 7.3 %gate_and_up.2 = (f32[16,48,128]{2,1,0:T(8,128)S(1)}, f32[16,48,128]{2,1,0:T(8,128)S(1)}, f32[3,128]{1,0:T(4,128)S(1)}, bf16[3,256,128]{2,1,0:T(8,128)(2,1)S(1)}, f32[16,48,128]{2,1,0:T(8,128)S(1)}) custom-call(s32[3]{0:T(128)S(1)} %pad_add_fusion.here, bf16[4,40,1024]{2,1,0:T(8,128)(2,1)S(1)} %line.1.refs_0_, ...), custom_call_target="tpu_custom_call" | custom-call | flops 1000000 | bytes 200000 | tf_op jit(solution)/shard_map/gate_and_up/pallas_call | solution.py:436
  31.9 1.2 %collective-permute-done.6.refs_1_ = bf16[4,40,1024]{2,1,0:T(8,128)(2,1)S(1)} collective-permute-done((bf16[4,40,1024]{2,1,0:T(8,128)(2,1)S(1)}, bf16[4,40,1024]{2,1,0:T(8,128)(2,1)S(1)}, u32[]{:S(2)}, u32[]{:S(2)}) %collective-permute-start.6) | collective-permute-done | bytes 327712 | tf_op jit(solution)/shard_map/ppermute | solution.py:162
  33.1 0.1 collective-permute-start.9
  33.2 3.3 %collective-permute-start = (bf16[8,128,128]{2,1,0:T(8,128)(2,1)S(1)}, bf16[8,128,128]{2,1,0:T(8,128)(2,1)S(1)}, u32[]{:S(2)}, u32[]{:S(2)}) collective-permute-start(bf16[8,128,128]{2,1,0:T(8,128)(2,1)S(1)} %get-tuple-element.15), channel_id=1, source_target_pairs={{0,16},{4,20},{8,24},{12,28},{16,0},{20,4},{24,8},{28,12},{1,17},{... | collective-permute-start | bytes 786440 | tf_op jit(solution)/shard_map/ppermute | solution.py:609
  36.5 7.3 %gate_and_up.3.own_ref = bf16[16,48,128]{2,1,0:T(8,128)(2,1)S(1)} custom-call(s32[3]{0:T(128)S(1)} %pad_add_fusion.here, bf16[8,40,1024]{2,1,0:T(8,128)(2,1)S(1)} %relay.2.refs_0_, bf16[8,40,1024]{2,1,0:T(8,128)(2,1)S(1)} %collective-permute-done.9.refs_1_, bf16[16,4096,128]{2,1,0:T(8,128)(2,1)} %refs_2_.1, bf16[16,4096,128]{2,1,0:T(8,128)(2,1)} %refs_3_.1, ...), custom_call_target="tpu_custom_call" | custom-call | flops 1000000 | bytes 200000 | tf_op jit(solution)/shard_map/gate_and_up/pallas_call | solution.py:436
  43.9 0.2 collective-permute-start.11
  44.2 1.5 %collective-permute-start.10 = (bf16[16,48,128]{2,1,0:T(8,128)(2,1)S(1)}, bf16[16,48,128]{2,1,0:T(8,128)(2,1)S(1)}, u32[]{:S(2)}, u32[]{:S(2)}) collective-permute-start(bf16[16,48,128]{2,1,0:T(8,128)(2,1)S(1)} %gate_and_up.3.own_ref), channel_id=1, source_target_pairs={{0,2},{1,3},{2,0},{3,1},{4,6},{5,7},{6,4},{7,5},{8,10},{9,11},{10,... | collective-permute-start | bytes 589832 | tf_op jit(solution)/shard_map/ppermute | solution.py:162
  45.7 3.3 %collective-permute-done.refs_0_.new_ref = bf16[8,128,128]{2,1,0:T(8,128)(2,1)S(1)} collective-permute-done((bf16[8,128,128]{2,1,0:T(8,128)(2,1)S(1)}, bf16[8,128,128]{2,1,0:T(8,128)(2,1)S(1)}, u32[]{:S(2)}, u32[]{:S(2)}) %collective-permute-start) | collective-permute-done | bytes 262176 | tf_op jit(solution)/shard_map/ppermute | solution.py:609
  49.0 5.0 %down.2.refs_1_.refs_0_ = f32[3,128,1024]{2,1,0:T(8,128)S(1)} custom-call(s32[3]{0:T(128)S(1)} %pad_add_fusion.here, bf16[16,48,128]{2,1,0:T(8,128)(2,1)S(1)} %gate_and_up.3.own_ref, bf16[16,48,128]{2,1,0:T(8,128)(2,1)S(1)} %collective-permute-done.11.other_ref, bf16[3,256,128]{2,1,0:T(8,128)(2,1)S(1)} %get-tuple-element.20.refs_7_.hot_ref, ...), custom_call_target="tpu_custom_call" | custom-call | flops 1000000 | bytes 100000 | tf_op jit(solution)/shard_map/down/pallas_call | solution.py:516
  54.0 0.1 collective-permute-start.12
  54.1 1.4 %collective-permute-done.12.other_ref = bf16[16,48,128]{2,1,0:T(8,128)(2,1)S(1)} collective-permute-done((bf16[16,48,128]{2,1,0:T(8,128)(2,1)S(1)}, bf16[16,48,128]{2,1,0:T(8,128)(2,1)S(1)}, u32[]{:S(2)}, u32[]{:S(2)}) %collective-permute-start.12) | collective-permute-done | bytes 196640 | tf_op jit(solution)/shard_map/ppermute | solution.py:162
  55.5 5.2 %down.3 = (bf16[4,288,128]{2,1,0:T(8,128)(2,1)S(1)}, bf16[4,288,128]{2,1,0:T(8,128)(2,1)S(1)}) custom-call(s32[3]{0:T(128)S(1)} %pad_add_fusion.here, bf16[16,48,128]{2,1,0:T(8,128)(2,1)S(1)} %relay.3.own_ref, bf16[16,48,128]{2,1,0:T(8,128)(2,1)S(1)} %collective-permute-done.12.other_ref, bf16[3,256,128]{2,1,0:T(8,128)(2,1)S(1)} %get-tuple-element.20.refs_7_.hot_ref, ...), custom_call_target="tpu_custom_call" | custom-call | flops 1000000 | bytes 100000 | tf_op jit(solution)/shard_map/down/pallas_call | solution.py:516
  60.8 1.6 %collective-permute-start.13 = (bf16[4,288,128]{2,1,0:T(8,128)(2,1)S(1)}, bf16[4,288,128]{2,1,0:T(8,128)(2,1)S(1)}, u32[]{:S(2)}, u32[]{:S(2)}) collective-permute-start(bf16[4,288,128]{2,1,0:T(8,128)(2,1)S(1)} %get-tuple-element.23), channel_id=1, source_target_pairs={{0,4},{4,0},{8,12},{12,8},{16,20},{20,16},{24,28},{28,24},{1,5},{5... | collective-permute-start | bytes 884744 | tf_op jit(solution)/shard_map/ppermute | solution.py:162
  62.5 5.5 %attention.2.tie.refs_0_ = bf16[3,12,2048]{2,1,0:T(8,128)(2,1)S(1)} custom-call(s32[4,12]{1,0:T(4,128)S(1)} %bitcast.13, s32[12]{0:T(128)S(1)} %copy-done.5, s32[8]{0:T(128)S(1)} %copy-done.6, bf16[3,12,2048]{2,1,0:T(8,128)(2,1)S(1)} %copy-done.1, bf16[3,12,128]{2,1,0:T(8,128)(2,1)S(1)} %copy-done.2, bf16[3,12,128]{2,1,0:T(8,128)(2,1)S(1)} %copy-done.3, ...), custom_call_target="tpu_custom_call" | custom-call | flops 400000000 | bytes 8000000 | tf_op jit(solution)/shard_map/attention/pallas_call | solution.py:143
  68.0 1.9 %collective-permute-done.13.got_ref = bf16[4,288,128]{2,1,0:T(8,128)(2,1)S(1)} collective-permute-done((bf16[4,288,128]{2,1,0:T(8,128)(2,1)S(1)}, bf16[4,288,128]{2,1,0:T(8,128)(2,1)S(1)}, u32[]{:S(2)}, u32[]{:S(2)}) %collective-permute-start.13) | collective-permute-done | bytes 294944 | tf_op jit(solution)/shard_map/ppermute | solution.py:162
  69.9 0.6 fold.1
  70.5 0.1 collective-permute-start.14
  70.6 2.1 %collective-permute-start.15 = (bf16[288,128]{1,0:T(8,128)(2,1)S(1)}, bf16[288,128]{1,0:T(8,128)(2,1)S(1)}, u32[]{:S(2)}, u32[]{:S(2)}) collective-permute-start(bf16[288,128]{1,0:T(8,128)(2,1)S(1)} %get-tuple-element.26), channel_id=1, source_target_pairs={{0,16},{4,20},{8,24},{12,28},{16,0},{20,4},{24,8},{28,12},{1,17},{... | collective-permute-start | bytes 221192 | tf_op jit(solution)/shard_map/ppermute | solution.py:162
  72.7 2.3 %collective-permute-start.16 = (bf16[288,128]{1,0:T(8,128)(2,1)S(1)}, bf16[288,128]{1,0:T(8,128)(2,1)S(1)}, u32[]{:S(2)}, u32[]{:S(2)}) collective-permute-start(bf16[288,128]{1,0:T(8,128)(2,1)S(1)} %get-tuple-element.27), channel_id=1, source_target_pairs={{0,24},{4,28},{8,16},{12,20},{16,8},{20,12},{24,0},{28,4},{1,25},{... | collective-permute-start | bytes 221192 | tf_op jit(solution)/shard_map/ppermute | solution.py:162
  75.0 3.0 %attention.3 = bf16[3,12,2048]{2,1,0:T(8,128)(2,1)} custom-call(s32[4,12]{1,0:T(4,128)S(1)} %bitcast.14, s32[12]{0:T(128)S(1)} %copy-done.5, s32[8]{0:T(128)S(1)} %copy-done.6, bf16[3,12,2048]{2,1,0:T(8,128)(2,1)S(1)} %copy-done.1, bf16[3,12,128]{2,1,0:T(8,128)(2,1)S(1)} %copy-done.2, bf16[3,12,128]{2,1,0:T(8,128)(2,1)S(1)} %copy-done.3, ...), custom_call_target="tpu_custom_call" | custom-call | flops 400000000 | bytes 8000000 | tf_op jit(solution)/shard_map/attention/pallas_call | solution.py:143
  78.0 1.0 %collective-permute-done.15.refs_1_ = bf16[288,128]{1,0:T(8,128)(2,1)S(1)} collective-permute-done((bf16[288,128]{1,0:T(8,128)(2,1)S(1)}, bf16[288,128]{1,0:T(8,128)(2,1)S(1)}, u32[]{:S(2)}, u32[]{:S(2)}) %collective-permute-start.15) | collective-permute-done | bytes 73760 | tf_op jit(solution)/shard_map/ppermute | solution.py:162
  79.0 0.7 finish.1
  (35 shorter events, 0.2 us)
Async XLA Ops:
  3.1 5.7 %collective-permute-start.1 = (bf16[40,1024]{1,0:T(8,128)(2,1)S(1)}, bf16[40,1024]{1,0:T(8,128)(2,1)S(1)}, u32[]{:S(2)}, u32[]{:S(2)}) collective-permute-start(bf16[40,1024]{1,0:T(8,128)(2,1)S(1)} %get-tuple-element.16.b0), channel_id=1, source_target_pairs={{0,8},{4,12},{8,0},{12,4},{16,24},{20,28},{24,16},{28,20},{1,9},{5... | collective-permute-start | bytes 245768 | tf_op jit(solution)/shard_map/ppermute | solution.py:162
  6.2 9.2 %collective-permute-start.2 = (bf16[40,1024]{1,0:T(8,128)(2,1)S(1)}, bf16[40,1024]{1,0:T(8,128)(2,1)S(1)}, u32[]{:S(2)}, u32[]{:S(2)}) collective-permute-start(bf16[40,1024]{1,0:T(8,128)(2,1)S(1)} %get-tuple-element.16.b0), channel_id=1, source_target_pairs={{0,16},{4,20},{8,24},{12,28},{16,0},{20,4},{24,8},{28,12},{1,17},{... | collective-permute-start | bytes 245768 | tf_op jit(solution)/shard_map/ppermute | solution.py:162
  8.7 6.6 %collective-permute-start.3 = (bf16[40,1024]{1,0:T(8,128)(2,1)S(1)}, bf16[40,1024]{1,0:T(8,128)(2,1)S(1)}, u32[]{:S(2)}, u32[]{:S(2)}) collective-permute-start(bf16[40,1024]{1,0:T(8,128)(2,1)S(1)} %get-tuple-element.16.b0), channel_id=1, source_target_pairs={{0,24},{4,28},{8,16},{12,20},{16,8},{20,12},{24,0},{28,4},{1,25},{... | collective-permute-start | bytes 245768 | tf_op jit(solution)/shard_map/ppermute | solution.py:162
  15.4 7.6 %collective-permute-start.5 = (bf16[4,40,1024]{2,1,0:T(8,128)(2,1)S(1)}, bf16[4,40,1024]{2,1,0:T(8,128)(2,1)S(1)}, u32[]{:S(2)}, u32[]{:S(2)}) collective-permute-start(bf16[4,40,1024]{2,1,0:T(8,128)(2,1)S(1)} %line.1.refs_0_), channel_id=1, source_target_pairs={{0,4},{4,0},{8,12},{12,8},{16,20},{20,16},{24,28},{28,24},{1,5},{5... | collective-permute-start | bytes 983048 | tf_op jit(solution)/shard_map/ppermute | solution.py:162
  17.0 7.5 %collective-permute-start.4 = (bf16[4,40,1024]{2,1,0:T(8,128)(2,1)S(1)}, bf16[4,40,1024]{2,1,0:T(8,128)(2,1)S(1)}, u32[]{:S(2)}, u32[]{:S(2)}) collective-permute-start(bf16[4,40,1024]{2,1,0:T(8,128)(2,1)S(1)} %line.1.refs_0_), channel_id=1, source_target_pairs={{0,2},{1,3},{2,0},{3,1},{4,6},{5,7},{6,4},{7,5},{8,10},{9,11},{10,... | collective-permute-start | bytes 983048 | tf_op jit(solution)/shard_map/ppermute | solution.py:162
  18.5 6.0 %collective-permute-start.7 = (bf16[4,40,1024]{2,1,0:T(8,128)(2,1)S(1)}, bf16[4,40,1024]{2,1,0:T(8,128)(2,1)S(1)}, u32[]{:S(2)}, u32[]{:S(2)}) collective-permute-start(bf16[4,40,1024]{2,1,0:T(8,128)(2,1)S(1)} %line.1.refs_0_), channel_id=1, source_target_pairs={{0,1},{1,0},{2,3},{3,2},{4,5},{5,4},{6,7},{7,6},{8,9},{9,8},{10,11... | collective-permute-start | bytes 983048 | tf_op jit(solution)/shard_map/ppermute | solution.py:162
  23.0 1.6 %collective-permute-start.8 = (bf16[4,40,1024]{2,1,0:T(8,128)(2,1)S(1)}, bf16[4,40,1024]{2,1,0:T(8,128)(2,1)S(1)}, u32[]{:S(2)}, u32[]{:S(2)}) collective-permute-start(bf16[4,40,1024]{2,1,0:T(8,128)(2,1)S(1)} %collective-permute-done.5.refs_1_), channel_id=1, source_target_pairs={{0,1},{1,0},{2,3},{3,2},{4,5},{5,4},{6,7},{7,6},{8,9},{9,8},{10,11... | collective-permute-start | bytes 983048 | tf_op jit(solution)/shard_map/ppermute | solution.py:162
  23.0 10.1 %collective-permute-start.6 = (bf16[4,40,1024]{2,1,0:T(8,128)(2,1)S(1)}, bf16[4,40,1024]{2,1,0:T(8,128)(2,1)S(1)}, u32[]{:S(2)}, u32[]{:S(2)}) collective-permute-start(bf16[4,40,1024]{2,1,0:T(8,128)(2,1)S(1)} %collective-permute-done.5.refs_1_), channel_id=1, source_target_pairs={{0,2},{1,3},{2,0},{3,1},{4,6},{5,7},{6,4},{7,5},{8,10},{9,11},{10,... | collective-permute-start | bytes 983048 | tf_op jit(solution)/shard_map/ppermute | solution.py:162
  33.1 3.4 %collective-permute-start.9 = (bf16[8,40,1024]{2,1,0:T(8,128)(2,1)S(1)}, bf16[8,40,1024]{2,1,0:T(8,128)(2,1)S(1)}, u32[]{:S(2)}, u32[]{:S(2)}) collective-permute-start(bf16[8,40,1024]{2,1,0:T(8,128)(2,1)S(1)} %relay.2.refs_0_), channel_id=1, source_target_pairs={{0,1},{1,0},{2,3},{3,2},{4,5},{5,4},{6,7},{7,6},{8,9},{9,8},{10,11... | collective-permute-start | bytes 1966088 | tf_op jit(solution)/shard_map/ppermute | solution.py:162
  33.2 15.8 %collective-permute-start = (bf16[8,128,128]{2,1,0:T(8,128)(2,1)S(1)}, bf16[8,128,128]{2,1,0:T(8,128)(2,1)S(1)}, u32[]{:S(2)}, u32[]{:S(2)}) collective-permute-start(bf16[8,128,128]{2,1,0:T(8,128)(2,1)S(1)} %get-tuple-element.15), channel_id=1, source_target_pairs={{0,16},{4,20},{8,24},{12,28},{16,0},{20,4},{24,8},{28,12},{1,17},{... | collective-permute-start | bytes 786440 | tf_op jit(solution)/shard_map/ppermute | solution.py:609
  43.8 18.6 %copy-start = (bf16[48,64,2,128]{3,2,1,0:T(2,128)(2,1)S(1)}, bf16[48,64,2,128]{3,2,1,0:T(2,128)(2,1)}, u32[]{:S(2)}) copy-start(bf16[48,64,2,128]{3,2,1,0:T(2,128)(2,1)} %param.24) | copy-start | bytes 4718596
  43.8 18.6 %copy-start.1 = (bf16[3,12,2048]{2,1,0:T(8,128)(2,1)S(1)}, bf16[3,12,2048]{2,1,0:T(8,128)(2,1)}, u32[]{:S(2)}) copy-start(bf16[3,12,2048]{2,1,0:T(8,128)(2,1)} %q_ref.3) | copy-start | bytes 442372
  43.8 18.6 %copy-start.2 = (bf16[3,12,128]{2,1,0:T(8,128)(2,1)S(1)}, bf16[3,12,128]{2,1,0:T(8,128)(2,1)}, u32[]{:S(2)}) copy-start(bf16[3,12,128]{2,1,0:T(8,128)(2,1)} %k_ref.3) | copy-start | bytes 27652
  43.9 18.6 %copy-start.3 = (bf16[3,12,128]{2,1,0:T(8,128)(2,1)S(1)}, bf16[3,12,128]{2,1,0:T(8,128)(2,1)}, u32[]{:S(2)}) copy-start(bf16[3,12,128]{2,1,0:T(8,128)(2,1)} %v_ref.3) | copy-start | bytes 27652
  43.9 18.5 %copy-start.4 = (s32[12,4]{0,1:T(4,128)S(1)}, s32[12,4]{0,1:T(4,128)}, u32[]{:S(2)}) copy-start(s32[12,4]{0,1:T(4,128)} %param.25) | copy-start | bytes 580
  43.9 18.5 %copy-start.5 = (s32[12]{0:T(128)S(1)}, s32[12]{0:T(128)}, u32[]{:S(2)}) copy-start(s32[12]{0:T(128)} %lengths.3) | copy-start | bytes 148
  43.9 18.5 %copy-start.6 = (s32[8]{0:T(128)S(1)}, s32[8]{0:T(128)}, u32[]{:S(2)}) copy-start(s32[8]{0:T(128)} %slots_in.3) | copy-start | bytes 100
  43.9 18.5 %copy-start.7 = (f32[128]{0:T(128)S(1)}, f32[128]{0:T(128)}, u32[]{:S(2)}) copy-start(f32[128]{0:T(128)} %param.22) | copy-start | bytes 1540
  43.9 18.5 %copy-start.8 = (f32[128]{0:T(128)S(1)}, f32[128]{0:T(128)}, u32[]{:S(2)}) copy-start(f32[128]{0:T(128)} %param.23) | copy-start | bytes 1540
  43.9 18.5 %copy-start.9 = (f32[1,128]{1,0:T(1,128)S(1)}, f32[1,128]{1,0:T(1,128)}, u32[]{:S(2)}) copy-start(f32[1,128]{1,0:T(1,128)} %constant.26.clone.speed_ref) | copy-start | bytes 1540
  43.9 5.1 %collective-permute-start.11 = (bf16[16,48,128]{2,1,0:T(8,128)(2,1)S(1)}, bf16[16,48,128]{2,1,0:T(8,128)(2,1)S(1)}, u32[]{:S(2)}, u32[]{:S(2)}) collective-permute-start(bf16[16,48,128]{2,1,0:T(8,128)(2,1)S(1)} %gate_and_up.3.own_ref), channel_id=1, source_target_pairs={{0,1},{1,0},{2,3},{3,2},{4,5},{5,4},{6,7},{7,6},{8,9},{9,8},{10,11... | collective-permute-start | bytes 589832 | tf_op jit(solution)/shard_map/ppermute | solution.py:162
  44.2 9.8 %collective-permute-start.10 = (bf16[16,48,128]{2,1,0:T(8,128)(2,1)S(1)}, bf16[16,48,128]{2,1,0:T(8,128)(2,1)S(1)}, u32[]{:S(2)}, u32[]{:S(2)}) collective-permute-start(bf16[16,48,128]{2,1,0:T(8,128)(2,1)S(1)} %gate_and_up.3.own_ref), channel_id=1, source_target_pairs={{0,2},{1,3},{2,0},{3,1},{4,6},{5,7},{6,4},{7,5},{8,10},{9,11},{10,... | collective-permute-start | bytes 589832 | tf_op jit(solution)/shard_map/ppermute | solution.py:162
  54.0 1.5 %collective-permute-start.12 = (bf16[16,48,128]{2,1,0:T(8,128)(2,1)S(1)}, bf16[16,48,128]{2,1,0:T(8,128)(2,1)S(1)}, u32[]{:S(2)}, u32[]{:S(2)}) collective-permute-start(bf16[16,48,128]{2,1,0:T(8,128)(2,1)S(1)} %relay.3.own_ref), channel_id=1, source_target_pairs={{0,1},{1,0},{2,3},{3,2},{4,5},{5,4},{6,7},{7,6},{8,9},{9,8},{10,11... | collective-permute-start | bytes 589832 | tf_op jit(solution)/shard_map/ppermute | solution.py:162
  60.8 9.1 %collective-permute-start.13 = (bf16[4,288,128]{2,1,0:T(8,128)(2,1)S(1)}, bf16[4,288,128]{2,1,0:T(8,128)(2,1)S(1)}, u32[]{:S(2)}, u32[]{:S(2)}) collective-permute-start(bf16[4,288,128]{2,1,0:T(8,128)(2,1)S(1)} %get-tuple-element.23), channel_id=1, source_target_pairs={{0,4},{4,0},{8,12},{12,8},{16,20},{20,16},{24,28},{28,24},{1,5},{5... | collective-permute-start | bytes 884744 | tf_op jit(solution)/shard_map/ppermute | solution.py:162
  70.5 7.5 %collective-permute-start.14 = (bf16[288,128]{1,0:T(8,128)(2,1)S(1)}, bf16[288,128]{1,0:T(8,128)(2,1)S(1)}, u32[]{:S(2)}, u32[]{:S(2)}) collective-permute-start(bf16[288,128]{1,0:T(8,128)(2,1)S(1)} %get-tuple-element.25), channel_id=1, source_target_pairs={{0,8},{4,12},{8,0},{12,4},{16,24},{20,28},{24,16},{28,20},{1,9},{5... | collective-permute-start | bytes 221192 | tf_op jit(solution)/shard_map/ppermute | solution.py:162
  70.6 8.4 %collective-permute-start.15 = (bf16[288,128]{1,0:T(8,128)(2,1)S(1)}, bf16[288,128]{1,0:T(8,128)(2,1)S(1)}, u32[]{:S(2)}, u32[]{:S(2)}) collective-permute-start(bf16[288,128]{1,0:T(8,128)(2,1)S(1)} %get-tuple-element.26), channel_id=1, source_target_pairs={{0,16},{4,20},{8,24},{12,28},{16,0},{20,4},{24,8},{28,12},{1,17},{... | collective-permute-start | bytes 221192 | tf_op jit(solution)/shard_map/ppermute | solution.py:162
  72.7 6.3 %collective-permute-start.16 = (bf16[288,128]{1,0:T(8,128)(2,1)S(1)}, bf16[288,128]{1,0:T(8,128)(2,1)S(1)}, u32[]{:S(2)}, u32[]{:S(2)}) collective-permute-start(bf16[288,128]{1,0:T(8,128)(2,1)S(1)} %get-tuple-element.27), channel_id=1, source_target_pairs={{0,24},{4,28},{8,16},{12,20},{16,8},{20,12},{24,0},{28,4},{1,25},{... | collective-permute-start | bytes 221192 | tf_op jit(solution)/shard_map/ppermute | solution.py:162

commit v2 on v1

--- a/solution.py
+++ b/solution.py
@@ -287,8 +287,7 @@
     count = len(pieces)
     if not first:
         line = refs[0].shape[0] // 2
-        blocks = [ref.at[pl.ds(at, line)] for ref in refs[:count] for at in (0, line)]
-        refs = refs[count:]
+        blocks, refs = [refs[0].at[pl.ds(at, line)] for at in (0, line)], refs[1:]
     else:
         blocks, refs = refs[: 2 * count], refs[2 * count :]
     wg_ref, wu_ref = refs[:2]
@@ -406,7 +405,7 @@
                 gate_ref[e] = gate
                 upper_ref[e] = upper
 
-    by_groups(shard_count, 2, copies, multiply)
+    by_groups(shard_count, 4 // count, copies, multiply)
 
 
 def up_pieces(pieces, here, blocks, w_gate, w_up, so_far=(), ties=()):
@@ -614,7 +613,8 @@
     )
     far = relay(far_own, far_other, tie=sums[2])
     last = swap(far, "rep", 1)
-    (hidden,) = up_pieces((2, 3), here, (far, last), w_gate, w_up, (*sums, hot, share))
+    sums = up_pieces((2,), here, (far,), w_gate, w_up, (*sums, hot))
+    (hidden,) = up_pieces((3,), here, (last,), w_gate, w_up, (*sums, hot, share))
     near = swap(hidden, "rep", 1)
     far = swap(hidden, "rep", 2)
     (sums,) = down_piece(0, here, hidden, near, hot, w_down, ties=(arriving,))

time: 79.9 us -> 79.9 us (level)
  Pallas kernels: 37.1 us -> 39.1 us
  waiting for transfers between devices: 20.1 us -> 18.1 us
    ppermute x1, waiting for transfers between devices: 3.33 us -> 1.36 us  [gathered(): lax.ppermute(leaving, 'dp', [(i, (i + ranks // 2) % ranks) for i in range...]
    pallas_call x2 -> x3, Pallas kernels: 14.7 us -> 16.6 us  [up_pieces(): pl.pallas_call(functools.partial(up_kernel, pieces), out_shape=out, in_sp...]
  transfers between devices with their start and end apart: 17 -> 17, of which waited for: 8 -> 8; matrix products, arithmetic and copies ran while one was open for 0% -> 0% of each run, Pallas kernels for 35% -> 38%
where the time goes in v2:
time: 79.9 us; the launch traced here: 79.7 us
  Pallas kernels  39.1 us (49%)
  starting transfers between devices  21.5 us (27%)
  waiting for transfers between devices  18.1 us (23%)
  between operations  0.91 us (1%)
    ppermute x16, starting transfers between devices, swap(): return lax.ppermute(x, axis, [(i, i ^ bits) for i in range(size)])  18.2 us
    ppermute x16, waiting for transfers between devices, swap(): return lax.ppermute(x, axis, [(i, i ^ bits) for i in range(size)])  16.7 us
    pallas_call x3, Pallas kernels, up_pieces(): pl.pallas_call(functools.partial(up_kernel, pieces), out_shape=out, in_sp...  16.6 us
    pallas_call x2, Pallas kernels, down_piece(): pl.pallas_call(functools.partial(down_kernel, piece), out_shape=out, in_s...  10.2 us
    pallas_call x2, Pallas kernels, attention(): pl.pallas_call(functools.partial(attention_kernel, first, count), out_sha...  8.53 us
    ppermute x1, starting transfers between devices, gathered(): lax.ppermute(leaving, 'dp', [(i, (i + ranks // 2) % ranks) for i in range...  3.28 us
    pallas_call x1, Pallas kernels, gathered(): pl.pallas_call(block_kernel, out_shape=(jax.ShapeDtypeStruct((tall, width...  2.34 us
  transfers between devices with their start and end apart: 17, of which 8 were waited for; matrix products, arithmetic and copies ran while one was open for 0% of the time, Pallas kernels for 38%

profile of v2, /device:TPU:0, one launch (start us, length us, event | category | flops | bytes accessed | tf_op | source)
XLA Modules:
  0.0 79.7 jit_solution(14410221825546805289)
XLA Ops:
  0.6 0.1 pad_add_fusion.here
  0.7 2.3 %token_block.1 = (bf16[40,1024]{1,0:T(8,128)(2,1)S(1)}, bf16[8,128,128]{2,1,0:T(8,128)(2,1)S(1)}) custom-call(s32[3]{0:T(128)S(1)} %pad_add_fusion.here, s32[8]{0:T(128)} %out_pages.1, s32[3,8,12]{2,1,0:T(8,128)} %bitcast.20, f32[3,8,12]{2,1,0:T(8,128)} %bitcast.21, bf16[3,12,1024]{2,1,0:T(8,128)(2,1)} %hidden_hbm.1, f32[1,4096]{1,0:T(1,128)} %bitcast.19, ...), custom_call_target="tpu_custom_call" | custom-call | tf_op jit(solution)/shard_map/token_block/pallas_call | solution.py:572
  3.1 3.1 %collective-permute-start.1 = (bf16[40,1024]{1,0:T(8,128)(2,1)S(1)}, bf16[40,1024]{1,0:T(8,128)(2,1)S(1)}, u32[]{:S(2)}, u32[]{:S(2)}) collective-permute-start(bf16[40,1024]{1,0:T(8,128)(2,1)S(1)} %get-tuple-element.19.b0), channel_id=1, source_target_pairs={{0,8},{4,12},{8,0},{12,4},{16,24},{20,28},{24,16},{28,20},{1,9},{5... | collective-permute-start | bytes 245768 | tf_op jit(solution)/shard_map/ppermute | solution.py:162
  6.2 2.6 %collective-permute-start.2 = (bf16[40,1024]{1,0:T(8,128)(2,1)S(1)}, bf16[40,1024]{1,0:T(8,128)(2,1)S(1)}, u32[]{:S(2)}, u32[]{:S(2)}) collective-permute-start(bf16[40,1024]{1,0:T(8,128)(2,1)S(1)} %get-tuple-element.19.b0), channel_id=1, source_target_pairs={{0,16},{4,20},{8,24},{12,28},{16,0},{20,4},{24,8},{28,12},{1,17},{... | collective-permute-start | bytes 245768 | tf_op jit(solution)/shard_map/ppermute | solution.py:162
  8.8 6.6 %collective-permute-done.2.b2 = bf16[40,1024]{1,0:T(8,128)(2,1)S(1)} collective-permute-done((bf16[40,1024]{1,0:T(8,128)(2,1)S(1)}, bf16[40,1024]{1,0:T(8,128)(2,1)S(1)}, u32[]{:S(2)}, u32[]{:S(2)}) %collective-permute-start.2) | collective-permute-done | bytes 81952 | tf_op jit(solution)/shard_map/ppermute | solution.py:162
  15.4 1.6 %collective-permute-start.5 = (bf16[4,40,1024]{2,1,0:T(8,128)(2,1)S(1)}, bf16[4,40,1024]{2,1,0:T(8,128)(2,1)S(1)}, u32[]{:S(2)}, u32[]{:S(2)}) collective-permute-start(bf16[4,40,1024]{2,1,0:T(8,128)(2,1)S(1)} %line.1.refs_0_), channel_id=1, source_target_pairs={{0,4},{4,0},{8,12},{12,8},{16,20},{20,16},{24,28},{28,24},{1,5},{5... | collective-permute-start | bytes 983048 | tf_op jit(solution)/shard_map/ppermute | solution.py:162
  17.0 1.5 %collective-permute-start.4 = (bf16[4,40,1024]{2,1,0:T(8,128)(2,1)S(1)}, bf16[4,40,1024]{2,1,0:T(8,128)(2,1)S(1)}, u32[]{:S(2)}, u32[]{:S(2)}) collective-permute-start(bf16[4,40,1024]{2,1,0:T(8,128)(2,1)S(1)} %line.1.refs_0_), channel_id=1, source_target_pairs={{0,2},{1,3},{2,0},{3,1},{4,6},{5,7},{6,4},{7,5},{8,10},{9,11},{10,... | collective-permute-start | bytes 983048 | tf_op jit(solution)/shard_map/ppermute | solution.py:162
  18.5 4.5 %collective-permute-done.5.refs_1_ = bf16[4,40,1024]{2,1,0:T(8,128)(2,1)S(1)} collective-permute-done((bf16[4,40,1024]{2,1,0:T(8,128)(2,1)S(1)}, bf16[4,40,1024]{2,1,0:T(8,128)(2,1)S(1)}, u32[]{:S(2)}, u32[]{:S(2)}) %collective-permute-start.5) | collective-permute-done | bytes 327712 | tf_op jit(solution)/shard_map/ppermute | solution.py:162
  23.0 1.5 %collective-permute-start.6 = (bf16[4,40,1024]{2,1,0:T(8,128)(2,1)S(1)}, bf16[4,40,1024]{2,1,0:T(8,128)(2,1)S(1)}, u32[]{:S(2)}, u32[]{:S(2)}) collective-permute-start(bf16[4,40,1024]{2,1,0:T(8,128)(2,1)S(1)} %collective-permute-done.5.refs_1_), channel_id=1, source_target_pairs={{0,2},{1,3},{2,0},{3,1},{4,6},{5,7},{6,4},{7,5},{8,10},{9,11},{10,... | collective-permute-start | bytes 983048 | tf_op jit(solution)/shard_map/ppermute | solution.py:162
  24.5 0.1 collective-permute-done.8.refs_3_
  24.6 7.3 %gate_and_up.3 = (f32[16,48,128]{2,1,0:T(8,128)S(1)}, f32[16,48,128]{2,1,0:T(8,128)S(1)}, f32[3,128]{1,0:T(4,128)S(1)}, bf16[3,256,128]{2,1,0:T(8,128)(2,1)S(1)}, f32[16,48,128]{2,1,0:T(8,128)S(1)}) custom-call(s32[3]{0:T(128)S(1)} %pad_add_fusion.here, bf16[4,40,1024]{2,1,0:T(8,128)(2,1)S(1)} %line.1.refs_0_, ...), custom_call_target="tpu_custom_call" | custom-call | flops 1000000 | bytes 200000 | tf_op jit(solution)/shard_map/gate_and_up/pallas_call | solution.py:435
  31.9 1.2 %collective-permute-done.6.refs_1_ = bf16[4,40,1024]{2,1,0:T(8,128)(2,1)S(1)} collective-permute-done((bf16[4,40,1024]{2,1,0:T(8,128)(2,1)S(1)}, bf16[4,40,1024]{2,1,0:T(8,128)(2,1)S(1)}, u32[]{:S(2)}, u32[]{:S(2)}) %collective-permute-start.6) | collective-permute-done | bytes 327712 | tf_op jit(solution)/shard_map/ppermute | solution.py:162
  33.1 0.1 collective-permute-start.9
  33.2 3.3 %collective-permute-start = (bf16[8,128,128]{2,1,0:T(8,128)(2,1)S(1)}, bf16[8,128,128]{2,1,0:T(8,128)(2,1)S(1)}, u32[]{:S(2)}, u32[]{:S(2)}) collective-permute-start(bf16[8,128,128]{2,1,0:T(8,128)(2,1)S(1)} %get-tuple-element.18), channel_id=1, source_target_pairs={{0,16},{4,20},{8,24},{12,28},{16,0},{20,4},{24,8},{28,12},{1,17},{... | collective-permute-start | bytes 786440 | tf_op jit(solution)/shard_map/ppermute | solution.py:608
  36.5 4.6 %gate_and_up.4 = (f32[16,48,128]{2,1,0:T(8,128)S(1)}, f32[16,48,128]{2,1,0:T(8,128)S(1)}, f32[3,128]{1,0:T(4,128)S(1)}) custom-call(s32[3]{0:T(128)S(1)} %pad_add_fusion.here, bf16[8,40,1024]{2,1,0:T(8,128)(2,1)S(1)} %relay.2.refs_0_, bf16[16,4096,128]{2,1,0:T(8,128)(2,1)} %refs_1_.3, bf16[16,4096,128]{2,1,0:T(8,128)(2,1)} %refs_2_.3, ...), custom_call_target="tpu_custom_call" | custom-call | flops 1000000 | bytes 100000 | tf_op jit(solution)/shard_map/gate_and_up/pallas_call | solution.py:435
  41.1 4.7 %gate_and_up.5.own_ref = bf16[16,48,128]{2,1,0:T(8,128)(2,1)S(1)} custom-call(s32[3]{0:T(128)S(1)} %pad_add_fusion.here, bf16[8,40,1024]{2,1,0:T(8,128)(2,1)S(1)} %collective-permute-done.9.refs_0_, bf16[16,4096,128]{2,1,0:T(8,128)(2,1)} %refs_1_.3, bf16[16,4096,128]{2,1,0:T(8,128)(2,1)} %refs_2_.3, f32[16,48,128]{2,1,0:T(8,128)S(1)} %get-tuple-element.24.refs_3_, ...), custom_call_target="tpu_custom_call" | custom-call | flops 1000000 | bytes 100000 | tf_op jit(solution)/shard_map/gate_and_up/pallas_call | solution.py:435
  45.9 0.2 collective-permute-start.11
  46.2 1.5 %collective-permute-start.10 = (bf16[16,48,128]{2,1,0:T(8,128)(2,1)S(1)}, bf16[16,48,128]{2,1,0:T(8,128)(2,1)S(1)}, u32[]{:S(2)}, u32[]{:S(2)}) collective-permute-start(bf16[16,48,128]{2,1,0:T(8,128)(2,1)S(1)} %gate_and_up.5.own_ref), channel_id=1, source_target_pairs={{0,2},{1,3},{2,0},{3,1},{4,6},{5,7},{6,4},{7,5},{8,10},{9,11},{10,... | collective-permute-start | bytes 589832 | tf_op jit(solution)/shard_map/ppermute | solution.py:162
  47.6 1.4 %collective-permute-done.refs_0_.new_ref = bf16[8,128,128]{2,1,0:T(8,128)(2,1)S(1)} collective-permute-done((bf16[8,128,128]{2,1,0:T(8,128)(2,1)S(1)}, bf16[8,128,128]{2,1,0:T(8,128)(2,1)S(1)}, u32[]{:S(2)}, u32[]{:S(2)}) %collective-permute-start) | collective-permute-done | bytes 262176 | tf_op jit(solution)/shard_map/ppermute | solution.py:608
  49.0 5.0 %down.2.refs_1_.refs_0_ = f32[3,128,1024]{2,1,0:T(8,128)S(1)} custom-call(s32[3]{0:T(128)S(1)} %pad_add_fusion.here, bf16[16,48,128]{2,1,0:T(8,128)(2,1)S(1)} %gate_and_up.5.own_ref, bf16[16,48,128]{2,1,0:T(8,128)(2,1)S(1)} %collective-permute-done.11.other_ref, bf16[3,256,128]{2,1,0:T(8,128)(2,1)S(1)} %get-tuple-element.23.refs_6_.hot_ref, ...), custom_call_target="tpu_custom_call" | custom-call | flops 1000000 | bytes 100000 | tf_op jit(solution)/shard_map/down/pallas_call | solution.py:515
  54.0 0.1 collective-permute-start.12
  54.1 1.4 %collective-permute-done.12.other_ref = bf16[16,48,128]{2,1,0:T(8,128)(2,1)S(1)} collective-permute-done((bf16[16,48,128]{2,1,0:T(8,128)(2,1)S(1)}, bf16[16,48,128]{2,1,0:T(8,128)(2,1)S(1)}, u32[]{:S(2)}, u32[]{:S(2)}) %collective-permute-start.12) | collective-permute-done | bytes 196640 | tf_op jit(solution)/shard_map/ppermute | solution.py:162
  55.5 5.2 %down.3 = (bf16[4,288,128]{2,1,0:T(8,128)(2,1)S(1)}, bf16[4,288,128]{2,1,0:T(8,128)(2,1)S(1)}) custom-call(s32[3]{0:T(128)S(1)} %pad_add_fusion.here, bf16[16,48,128]{2,1,0:T(8,128)(2,1)S(1)} %relay.3.own_ref, bf16[16,48,128]{2,1,0:T(8,128)(2,1)S(1)} %collective-permute-done.12.other_ref, bf16[3,256,128]{2,1,0:T(8,128)(2,1)S(1)} %get-tuple-element.23.refs_6_.hot_ref, ...), custom_call_target="tpu_custom_call" | custom-call | flops 1000000 | bytes 100000 | tf_op jit(solution)/shard_map/down/pallas_call | solution.py:515
  60.8 1.6 %collective-permute-start.13 = (bf16[4,288,128]{2,1,0:T(8,128)(2,1)S(1)}, bf16[4,288,128]{2,1,0:T(8,128)(2,1)S(1)}, u32[]{:S(2)}, u32[]{:S(2)}) collective-permute-start(bf16[4,288,128]{2,1,0:T(8,128)(2,1)S(1)} %get-tuple-element.29), channel_id=1, source_target_pairs={{0,4},{4,0},{8,12},{12,8},{16,20},{20,16},{24,28},{28,24},{1,5},{5... | collective-permute-start | bytes 884744 | tf_op jit(solution)/shard_map/ppermute | solution.py:162
  62.5 5.5 %attention.2.tie.refs_0_ = bf16[3,12,2048]{2,1,0:T(8,128)(2,1)S(1)} custom-call(s32[4,12]{1,0:T(4,128)S(1)} %bitcast.13, s32[12]{0:T(128)S(1)} %copy-done.5, s32[8]{0:T(128)S(1)} %copy-done.6, bf16[3,12,2048]{2,1,0:T(8,128)(2,1)S(1)} %copy-done.1, bf16[3,12,128]{2,1,0:T(8,128)(2,1)S(1)} %copy-done.2, bf16[3,12,128]{2,1,0:T(8,128)(2,1)S(1)} %copy-done.3, ...), custom_call_target="tpu_custom_call" | custom-call | flops 400000000 | bytes 8000000 | tf_op jit(solution)/shard_map/attention/pallas_call | solution.py:143
  68.0 1.9 %collective-permute-done.13.got_ref = bf16[4,288,128]{2,1,0:T(8,128)(2,1)S(1)} collective-permute-done((bf16[4,288,128]{2,1,0:T(8,128)(2,1)S(1)}, bf16[4,288,128]{2,1,0:T(8,128)(2,1)S(1)}, u32[]{:S(2)}, u32[]{:S(2)}) %collective-permute-start.13) | collective-permute-done | bytes 294944 | tf_op jit(solution)/shard_map/ppermute | solution.py:162
  69.9 0.6 fold.1
  70.6 2.1 %collective-permute-start.15 = (bf16[288,128]{1,0:T(8,128)(2,1)S(1)}, bf16[288,128]{1,0:T(8,128)(2,1)S(1)}, u32[]{:S(2)}, u32[]{:S(2)}) collective-permute-start(bf16[288,128]{1,0:T(8,128)(2,1)S(1)} %get-tuple-element.32), channel_id=1, source_target_pairs={{0,16},{4,20},{8,24},{12,28},{16,0},{20,4},{24,8},{28,12},{1,17},{... | collective-permute-start | bytes 221192 | tf_op jit(solution)/shard_map/ppermute | solution.py:162
  72.7 2.3 %collective-permute-start.16 = (bf16[288,128]{1,0:T(8,128)(2,1)S(1)}, bf16[288,128]{1,0:T(8,128)(2,1)S(1)}, u32[]{:S(2)}, u32[]{:S(2)}) collective-permute-start(bf16[288,128]{1,0:T(8,128)(2,1)S(1)} %get-tuple-element.33), channel_id=1, source_target_pairs={{0,24},{4,28},{8,16},{12,20},{16,8},{20,12},{24,0},{28,4},{1,25},{... | collective-permute-start | bytes 221192 | tf_op jit(solution)/shard_map/ppermute | solution.py:162
  75.0 3.0 %attention.3 = bf16[3,12,2048]{2,1,0:T(8,128)(2,1)} custom-call(s32[4,12]{1,0:T(4,128)S(1)} %bitcast.14, s32[12]{0:T(128)S(1)} %copy-done.5, s32[8]{0:T(128)S(1)} %copy-done.6, bf16[3,12,2048]{2,1,0:T(8,128)(2,1)S(1)} %copy-done.1, bf16[3,12,128]{2,1,0:T(8,128)(2,1)S(1)} %copy-done.2, bf16[3,12,128]{2,1,0:T(8,128)(2,1)S(1)} %copy-done.3, ...), custom_call_target="tpu_custom_call" | custom-call | flops 400000000 | bytes 8000000 | tf_op jit(solution)/shard_map/attention/pallas_call | solution.py:143
  78.0 1.0 %collective-permute-done.15.refs_1_ = bf16[288,128]{1,0:T(8,128)(2,1)S(1)} collective-permute-done((bf16[288,128]{1,0:T(8,128)(2,1)S(1)}, bf16[288,128]{1,0:T(8,128)(2,1)S(1)}, u32[]{:S(2)}, u32[]{:S(2)}) %collective-permute-start.15) | collective-permute-done | bytes 73760 | tf_op jit(solution)/shard_map/ppermute | solution.py:162
  79.0 0.7 finish.1
  (36 shorter events, 0.2 us)
Async XLA Ops:
  3.1 5.7 %collective-permute-start.1 = (bf16[40,1024]{1,0:T(8,128)(2,1)S(1)}, bf16[40,1024]{1,0:T(8,128)(2,1)S(1)}, u32[]{:S(2)}, u32[]{:S(2)}) collective-permute-start(bf16[40,1024]{1,0:T(8,128)(2,1)S(1)} %get-tuple-element.19.b0), channel_id=1, source_target_pairs={{0,8},{4,12},{8,0},{12,4},{16,24},{20,28},{24,16},{28,20},{1,9},{5... | collective-permute-start | bytes 245768 | tf_op jit(solution)/shard_map/ppermute | solution.py:162
  6.2 9.2 %collective-permute-start.2 = (bf16[40,1024]{1,0:T(8,128)(2,1)S(1)}, bf16[40,1024]{1,0:T(8,128)(2,1)S(1)}, u32[]{:S(2)}, u32[]{:S(2)}) collective-permute-start(bf16[40,1024]{1,0:T(8,128)(2,1)S(1)} %get-tuple-element.19.b0), channel_id=1, source_target_pairs={{0,16},{4,20},{8,24},{12,28},{16,0},{20,4},{24,8},{28,12},{1,17},{... | collective-permute-start | bytes 245768 | tf_op jit(solution)/shard_map/ppermute | solution.py:162
  8.7 6.6 %collective-permute-start.3 = (bf16[40,1024]{1,0:T(8,128)(2,1)S(1)}, bf16[40,1024]{1,0:T(8,128)(2,1)S(1)}, u32[]{:S(2)}, u32[]{:S(2)}) collective-permute-start(bf16[40,1024]{1,0:T(8,128)(2,1)S(1)} %get-tuple-element.19.b0), channel_id=1, source_target_pairs={{0,24},{4,28},{8,16},{12,20},{16,8},{20,12},{24,0},{28,4},{1,25},{... | collective-permute-start | bytes 245768 | tf_op jit(solution)/shard_map/ppermute | solution.py:162
  15.4 7.6 %collective-permute-start.5 = (bf16[4,40,1024]{2,1,0:T(8,128)(2,1)S(1)}, bf16[4,40,1024]{2,1,0:T(8,128)(2,1)S(1)}, u32[]{:S(2)}, u32[]{:S(2)}) collective-permute-start(bf16[4,40,1024]{2,1,0:T(8,128)(2,1)S(1)} %line.1.refs_0_), channel_id=1, source_target_pairs={{0,4},{4,0},{8,12},{12,8},{16,20},{20,16},{24,28},{28,24},{1,5},{5... | collective-permute-start | bytes 983048 | tf_op jit(solution)/shard_map/ppermute | solution.py:162
  17.0 7.5 %collective-permute-start.4 = (bf16[4,40,1024]{2,1,0:T(8,128)(2,1)S(1)}, bf16[4,40,1024]{2,1,0:T(8,128)(2,1)S(1)}, u32[]{:S(2)}, u32[]{:S(2)}) collective-permute-start(bf16[4,40,1024]{2,1,0:T(8,128)(2,1)S(1)} %line.1.refs_0_), channel_id=1, source_target_pairs={{0,2},{1,3},{2,0},{3,1},{4,6},{5,7},{6,4},{7,5},{8,10},{9,11},{10,... | collective-permute-start | bytes 983048 | tf_op jit(solution)/shard_map/ppermute | solution.py:162
  18.5 6.0 %collective-permute-start.7 = (bf16[4,40,1024]{2,1,0:T(8,128)(2,1)S(1)}, bf16[4,40,1024]{2,1,0:T(8,128)(2,1)S(1)}, u32[]{:S(2)}, u32[]{:S(2)}) collective-permute-start(bf16[4,40,1024]{2,1,0:T(8,128)(2,1)S(1)} %line.1.refs_0_), channel_id=1, source_target_pairs={{0,1},{1,0},{2,3},{3,2},{4,5},{5,4},{6,7},{7,6},{8,9},{9,8},{10,11... | collective-permute-start | bytes 983048 | tf_op jit(solution)/shard_map/ppermute | solution.py:162
  23.0 1.6 %collective-permute-start.8 = (bf16[4,40,1024]{2,1,0:T(8,128)(2,1)S(1)}, bf16[4,40,1024]{2,1,0:T(8,128)(2,1)S(1)}, u32[]{:S(2)}, u32[]{:S(2)}) collective-permute-start(bf16[4,40,1024]{2,1,0:T(8,128)(2,1)S(1)} %collective-permute-done.5.refs_1_), channel_id=1, source_target_pairs={{0,1},{1,0},{2,3},{3,2},{4,5},{5,4},{6,7},{7,6},{8,9},{9,8},{10,11... | collective-permute-start | bytes 983048 | tf_op jit(solution)/shard_map/ppermute | solution.py:162
  23.0 10.1 %collective-permute-start.6 = (bf16[4,40,1024]{2,1,0:T(8,128)(2,1)S(1)}, bf16[4,40,1024]{2,1,0:T(8,128)(2,1)S(1)}, u32[]{:S(2)}, u32[]{:S(2)}) collective-permute-start(bf16[4,40,1024]{2,1,0:T(8,128)(2,1)S(1)} %collective-permute-done.5.refs_1_), channel_id=1, source_target_pairs={{0,2},{1,3},{2,0},{3,1},{4,6},{5,7},{6,4},{7,5},{8,10},{9,11},{10,... | collective-permute-start | bytes 983048 | tf_op jit(solution)/shard_map/ppermute | solution.py:162
  33.1 8.0 %collective-permute-start.9 = (bf16[8,40,1024]{2,1,0:T(8,128)(2,1)S(1)}, bf16[8,40,1024]{2,1,0:T(8,128)(2,1)S(1)}, u32[]{:S(2)}, u32[]{:S(2)}) collective-permute-start(bf16[8,40,1024]{2,1,0:T(8,128)(2,1)S(1)} %relay.2.refs_0_), channel_id=1, source_target_pairs={{0,1},{1,0},{2,3},{3,2},{4,5},{5,4},{6,7},{7,6},{8,9},{9,8},{10,11... | collective-permute-start | bytes 1966088 | tf_op jit(solution)/shard_map/ppermute | solution.py:162
  33.2 15.8 %collective-permute-start = (bf16[8,128,128]{2,1,0:T(8,128)(2,1)S(1)}, bf16[8,128,128]{2,1,0:T(8,128)(2,1)S(1)}, u32[]{:S(2)}, u32[]{:S(2)}) collective-permute-start(bf16[8,128,128]{2,1,0:T(8,128)(2,1)S(1)} %get-tuple-element.18), channel_id=1, source_target_pairs={{0,16},{4,20},{8,24},{12,28},{16,0},{20,4},{24,8},{28,12},{1,17},{... | collective-permute-start | bytes 786440 | tf_op jit(solution)/shard_map/ppermute | solution.py:608
  45.8 16.6 %copy-start = (bf16[48,64,2,128]{3,2,1,0:T(2,128)(2,1)S(1)}, bf16[48,64,2,128]{3,2,1,0:T(2,128)(2,1)}, u32[]{:S(2)}) copy-start(bf16[48,64,2,128]{3,2,1,0:T(2,128)(2,1)} %param.24) | copy-start | bytes 4718596
  45.8 16.6 %copy-start.1 = (bf16[3,12,2048]{2,1,0:T(8,128)(2,1)S(1)}, bf16[3,12,2048]{2,1,0:T(8,128)(2,1)}, u32[]{:S(2)}) copy-start(bf16[3,12,2048]{2,1,0:T(8,128)(2,1)} %q_ref.3) | copy-start | bytes 442372
  45.8 16.6 %copy-start.2 = (bf16[3,12,128]{2,1,0:T(8,128)(2,1)S(1)}, bf16[3,12,128]{2,1,0:T(8,128)(2,1)}, u32[]{:S(2)}) copy-start(bf16[3,12,128]{2,1,0:T(8,128)(2,1)} %k_ref.3) | copy-start | bytes 27652
  45.8 16.6 %copy-start.3 = (bf16[3,12,128]{2,1,0:T(8,128)(2,1)S(1)}, bf16[3,12,128]{2,1,0:T(8,128)(2,1)}, u32[]{:S(2)}) copy-start(bf16[3,12,128]{2,1,0:T(8,128)(2,1)} %v_ref.3) | copy-start | bytes 27652
  45.8 16.6 %copy-start.4 = (s32[12,4]{0,1:T(4,128)S(1)}, s32[12,4]{0,1:T(4,128)}, u32[]{:S(2)}) copy-start(s32[12,4]{0,1:T(4,128)} %param.25) | copy-start | bytes 580
  45.9 16.6 %copy-start.5 = (s32[12]{0:T(128)S(1)}, s32[12]{0:T(128)}, u32[]{:S(2)}) copy-start(s32[12]{0:T(128)} %lengths.3) | copy-start | bytes 148
  45.9 16.6 %copy-start.6 = (s32[8]{0:T(128)S(1)}, s32[8]{0:T(128)}, u32[]{:S(2)}) copy-start(s32[8]{0:T(128)} %slots_in.3) | copy-start | bytes 100
  45.9 16.6 %copy-start.7 = (f32[128]{0:T(128)S(1)}, f32[128]{0:T(128)}, u32[]{:S(2)}) copy-start(f32[128]{0:T(128)} %param.22) | copy-start | bytes 1540
  45.9 16.6 %copy-start.8 = (f32[128]{0:T(128)S(1)}, f32[128]{0:T(128)}, u32[]{:S(2)}) copy-start(f32[128]{0:T(128)} %param.23) | copy-start | bytes 1540
  45.9 16.6 %copy-start.9 = (f32[1,128]{1,0:T(1,128)S(1)}, f32[1,128]{1,0:T(1,128)}, u32[]{:S(2)}) copy-start(f32[1,128]{1,0:T(1,128)} %constant.26.clone.speed_ref) | copy-start | bytes 1540
  45.9 3.1 %collective-permute-start.11 = (bf16[16,48,128]{2,1,0:T(8,128)(2,1)S(1)}, bf16[16,48,128]{2,1,0:T(8,128)(2,1)S(1)}, u32[]{:S(2)}, u32[]{:S(2)}) collective-permute-start(bf16[16,48,128]{2,1,0:T(8,128)(2,1)S(1)} %gate_and_up.5.own_ref), channel_id=1, source_target_pairs={{0,1},{1,0},{2,3},{3,2},{4,5},{5,4},{6,7},{7,6},{8,9},{9,8},{10,11... | collective-permute-start | bytes 589832 | tf_op jit(solution)/shard_map/ppermute | solution.py:162
  46.2 7.8 %collective-permute-start.10 = (bf16[16,48,128]{2,1,0:T(8,128)(2,1)S(1)}, bf16[16,48,128]{2,1,0:T(8,128)(2,1)S(1)}, u32[]{:S(2)}, u32[]{:S(2)}) collective-permute-start(bf16[16,48,128]{2,1,0:T(8,128)(2,1)S(1)} %gate_and_up.5.own_ref), channel_id=1, source_target_pairs={{0,2},{1,3},{2,0},{3,1},{4,6},{5,7},{6,4},{7,5},{8,10},{9,11},{10,... | collective-permute-start | bytes 589832 | tf_op jit(solution)/shard_map/ppermute | solution.py:162
  54.0 1.5 %collective-permute-start.12 = (bf16[16,48,128]{2,1,0:T(8,128)(2,1)S(1)}, bf16[16,48,128]{2,1,0:T(8,128)(2,1)S(1)}, u32[]{:S(2)}, u32[]{:S(2)}) collective-permute-start(bf16[16,48,128]{2,1,0:T(8,128)(2,1)S(1)} %relay.3.own_ref), channel_id=1, source_target_pairs={{0,1},{1,0},{2,3},{3,2},{4,5},{5,4},{6,7},{7,6},{8,9},{9,8},{10,11... | collective-permute-start | bytes 589832 | tf_op jit(solution)/shard_map/ppermute | solution.py:162
  60.8 9.1 %collective-permute-start.13 = (bf16[4,288,128]{2,1,0:T(8,128)(2,1)S(1)}, bf16[4,288,128]{2,1,0:T(8,128)(2,1)S(1)}, u32[]{:S(2)}, u32[]{:S(2)}) collective-permute-start(bf16[4,288,128]{2,1,0:T(8,128)(2,1)S(1)} %get-tuple-element.29), channel_id=1, source_target_pairs={{0,4},{4,0},{8,12},{12,8},{16,20},{20,16},{24,28},{28,24},{1,5},{5... | collective-permute-start | bytes 884744 | tf_op jit(solution)/shard_map/ppermute | solution.py:162
  70.5 7.5 %collective-permute-start.14 = (bf16[288,128]{1,0:T(8,128)(2,1)S(1)}, bf16[288,128]{1,0:T(8,128)(2,1)S(1)}, u32[]{:S(2)}, u32[]{:S(2)}) collective-permute-start(bf16[288,128]{1,0:T(8,128)(2,1)S(1)} %get-tuple-element.31), channel_id=1, source_target_pairs={{0,8},{4,12},{8,0},{12,4},{16,24},{20,28},{24,16},{28,20},{1,9},{5... | collective-permute-start | bytes 221192 | tf_op jit(solution)/shard_map/ppermute | solution.py:162
  70.6 8.4 %collective-permute-start.15 = (bf16[288,128]{1,0:T(8,128)(2,1)S(1)}, bf16[288,128]{1,0:T(8,128)(2,1)S(1)}, u32[]{:S(2)}, u32[]{:S(2)}) collective-permute-start(bf16[288,128]{1,0:T(8,128)(2,1)S(1)} %get-tuple-element.32), channel_id=1, source_target_pairs={{0,16},{4,20},{8,24},{12,28},{16,0},{20,4},{24,8},{28,12},{1,17},{... | collective-permute-start | bytes 221192 | tf_op jit(solution)/shard_map/ppermute | solution.py:162
  72.7 6.3 %collective-permute-start.16 = (bf16[288,128]{1,0:T(8,128)(2,1)S(1)}, bf16[288,128]{1,0:T(8,128)(2,1)S(1)}, u32[]{:S(2)}, u32[]{:S(2)}) collective-permute-start(bf16[288,128]{1,0:T(8,128)(2,1)S(1)} %get-tuple-element.33), channel_id=1, source_target_pairs={{0,24},{4,28},{8,16},{12,20},{16,8},{20,12},{24,0},{28,4},{1,25},{... | collective-permute-start | bytes 221192 | tf_op jit(solution)/shard_map/ppermute | solution.py:162
